TPU v7x, 32 devices: a whole 2x2x4 slice. The times are simulated.
32 devices in a mesh: dp: 8 (over z, y), group: 4 (over x, core).
Axes of the slice: x: 2, y: 2, z: 4, core: 2. Of those that a mesh axis runs over, the one named last changes fastest.
Arguments:
- features: bfloat16 [65536, 602], P(('dp', 'group')), may hold values from -6.7 to 6.7
- labels: int32 [65536], P(('dp', 'group')), may hold values from 0 to 40
- neighbors: int32 [65536, 8], P(('dp', 'group')), may hold values from 0 to 2047
- degree: int32 [65536], P(('dp', 'group')), may hold values from 1 to 8
- node_counts: int32 [65536], P(('dp', 'group')), may hold values from 1 to 72, as said below
- edge_counts: int32 [65536, 8], P(('dp', 'group')), may hold values from 1 to 8
- live_nodes: int32 [32], P(('dp', 'group')), may hold values from 1365 to 2048, as said below
- input_weight: float32 [602, 512], P(None, ('dp', 'group')), may hold values from -0.25 to 0.25
- pair_weight: float32 [3, 512, 1024], P(None, None, ('dp', 'group')), may hold values from -0.25 to 0.25
- proj_weight: float32 [3, 1024, 512], P(None, ('dp', 'group')), may hold values from -0.1875 to 0.1875
- head_weight: float32 [512, 41], P(('dp', 'group')), may hold values from -0.25 to 0.25
- input_first: float32 [602, 512], P(None, ('dp', 'group')), may hold values from -0.0024414062 to 0.0024414062
- pair_first: float32 [3, 512, 1024], P(None, None, ('dp', 'group')), may hold values from -0.0024414062 to 0.0024414062
- proj_first: float32 [3, 1024, 512], P(None, ('dp', 'group')), may hold values from -0.0024414062 to 0.0024414062
- head_first: float32 [512, 41], P(('dp', 'group')), may hold values from -0.0078125 to 0.0078125
- input_second: float32 [602, 512], P(None, ('dp', 'group')), may hold values from 2.4414062e-08 to 1.953125e-07
- pair_second: float32 [3, 512, 1024], P(None, None, ('dp', 'group')), may hold values from 2.4414062e-08 to 1.953125e-07
- proj_second: float32 [3, 1024, 512], P(None, ('dp', 'group')), may hold values from 2.4414062e-08 to 1.953125e-07
- head_second: float32 [512, 41], P(('dp', 'group')), may hold values from 3.4332277e-07 to 2.7465821e-06
Outputs:
- mean_loss: float32 [], replicated
- weight_mean: float32 [], replicated
- input_new: float32 [602, 512], P(None, ('dp', 'group'))
- pair_new: float32 [3, 512, 1024], P(None, None, ('dp', 'group'))
- proj_new: float32 [3, 1024, 512], P(None, ('dp', 'group'))
- head_new: float32 [512, 41], P(('dp', 'group'))
- input_first_new: float32 [602, 512], P(None, ('dp', 'group'))
- pair_first_new: float32 [3, 512, 1024], P(None, None, ('dp', 'group'))
- proj_first_new: float32 [3, 1024, 512], P(None, ('dp', 'group'))
- head_first_new: float32 [512, 41], P(('dp', 'group'))
- input_second_new: float32 [602, 512], P(None, ('dp', 'group'))
- pair_second_new: float32 [3, 512, 1024], P(None, None, ('dp', 'group'))
- proj_second_new: float32 [3, 1024, 512], P(None, ('dp', 'group'))
- head_second_new: float32 [512, 41], P(('dp', 'group'))
- input_copy: bfloat16 [602, 512], P(None, ('dp', 'group'))
- pair_copy: bfloat16 [3, 512, 1024], P(None, None, ('dp', 'group'))
- proj_copy: bfloat16 [3, 1024, 512], P(None, ('dp', 'group'))
- head_copy: bfloat16 [512, 41], P(('dp', 'group'))
Inputs may be any that keep to these rules, and one draw needn't show every extreme that they name: `node_counts`: each subgraph's counts are a random base of 1 to 8 times a factor of 1 to 3 that grows with the subgraph's index along dp, times another of 1 to 3 that grows with its index along group. `live_nodes`: some subgraph has exactly 2048 real nodes and some exactly (4096) // 3.
All inputs are finite; a program needn't handle non-finite values.
Results may differ from a plain program's by a relative error of at most 0.0049.
The roundings to bfloat16 on the way count: a program that leaves them out, or rounds other values in their place, can miss the bound.
Values may be sent and summed in bfloat16 or wider, within the bound.
A program may use at most 192 MiB of HBM per device.

v0:
```python
import jax
import jax.numpy as jnp
from jax import lax
from jax.sharding import PartitionSpec as P

LAYERS = 3
STEP = 5


learn_rate = 0.03
beta_first = 0.5
beta_second = 0.5
adam_eps = 1e-08
decay_rate = 0.01
norm_eps = 1e-06


def normalize(preact):
    active = jax.nn.gelu(preact)
    return active * lax.rsqrt(jnp.mean(active * active, axis=-1, keepdims=True) + norm_eps)


def slot_terms(neighbors, degree, live_count):
    count_nodes, fanout = neighbors.shape
    node_live = jnp.arange(count_nodes, dtype=jnp.int32) < live_count
    used = (
        (jnp.arange(fanout, dtype=jnp.int32)[None, :] < degree[:, None])
        & (neighbors < live_count)
        & node_live[:, None]
    )
    return (node_live, used)


def coefficients(used, node_counts, edge_counts, total_node, total_edge):
    node_float = node_counts.astype(jnp.float32)
    edge_float = edge_counts.astype(jnp.float32)
    spread = jnp.maximum(jnp.sum(used.astype(jnp.float32), axis=1), 1.0)
    value = node_float[:, None] * total_edge / (edge_float * total_node * spread[:, None])
    return jnp.where(used, value, 0.0)


def contract_rows(left, right):
    return lax.dot_general(
        left, right, (((0,), (0,)), ((), ())), preferred_element_type=jnp.float32
    )


def contract_cols(left, right):
    return lax.dot_general(
        left, right, (((1,), (1,)), ((), ())), preferred_element_type=jnp.float32
    )


def coef_matrix(neighbors, coefs):
    count_nodes = neighbors.shape[0]
    columns = lax.iota(jnp.int32, count_nodes)[None, :]
    matrix = jnp.zeros((count_nodes, count_nodes), jnp.float32)
    for neighbor_slot in range(neighbors.shape[1]):
        matrix = matrix + jnp.where(
            neighbors[:, neighbor_slot : neighbor_slot + 1] == columns,
            coefs[:, neighbor_slot : neighbor_slot + 1],
            0.0,
        )
    return matrix


def layer_forward(hidden, pair_w, proj_w, matrix):
    width = pair_w.shape[0]
    pooled = jnp.dot(
        matrix,
        hidden.astype(jnp.float32),
        precision=lax.Precision.HIGHEST,
        preferred_element_type=jnp.float32,
    ).astype(jnp.bfloat16)
    self_part = jnp.dot(hidden, pair_w[:, :width], preferred_element_type=jnp.float32)
    nbr_part = jnp.dot(pooled, pair_w[:, width:], preferred_element_type=jnp.float32)
    joined = jnp.concatenate([self_part, nbr_part], axis=1).astype(jnp.bfloat16)
    preact = jnp.dot(joined, proj_w, preferred_element_type=jnp.float32)
    return (normalize(preact).astype(jnp.bfloat16), (hidden, pooled, joined, preact))


def layer_backward(grad_out, saved, pair_w, proj_w, matrix):
    hidden, pooled, joined, preact = saved
    width = pair_w.shape[0]
    _, pullback = jax.vjp(normalize, preact)
    grad_preact = pullback(grad_out)[0].astype(jnp.bfloat16)
    grad_proj = contract_rows(joined, grad_preact)
    grad_joined = contract_cols(grad_preact, proj_w).astype(jnp.bfloat16)
    grad_pair = jnp.concatenate(
        [
            contract_rows(hidden, grad_joined[:, :width]),
            contract_rows(pooled, grad_joined[:, width:]),
        ],
        axis=1,
    )
    grad_hidden = contract_cols(grad_joined[:, :width], pair_w[:, :width])
    grad_pooled = contract_cols(grad_joined[:, width:], pair_w[:, width:])
    grad_hidden = grad_hidden + lax.dot_general(
        matrix,
        grad_pooled,
        (((0,), (0,)), ((), ())),
        precision=lax.Precision.HIGHEST,
        preferred_element_type=jnp.float32,
    )
    return (grad_hidden, grad_pair, grad_proj)


def adamw_update(weight, first, second, grad):
    first_new = beta_first * first + (1.0 - beta_first) * grad
    second_new = beta_second * second + (1.0 - beta_second) * grad * grad
    first_hat = first_new / (1.0 - beta_first**STEP)
    second_hat = second_new / (1.0 - beta_second**STEP)
    weight_new = weight - learn_rate * (
        first_hat / (jnp.sqrt(second_hat) + adam_eps) + decay_rate * weight
    )
    return (weight_new, first_new, second_new)


def body(
    features,
    labels,
    neighbors,
    degree,
    node_counts,
    edge_counts,
    live_nodes,
    input_weight,
    pair_weight,
    proj_weight,
    head_weight,
    input_first,
    pair_first,
    proj_first,
    head_first,
    input_second,
    pair_second,
    proj_second,
    head_second,
):
    count_nodes = features.shape[0]
    all_nodes = jnp.float32(count_nodes * lax.axis_size(("dp", "group")))
    node_live, used = slot_terms(neighbors, degree, live_nodes[0])
    node_float = node_counts.astype(jnp.float32)
    node_local = jnp.sum(jnp.where(node_live, node_float, 0.0))
    edge_local = jnp.sum(jnp.where(used, edge_counts.astype(jnp.float32), 0.0))
    total_node, total_edge = lax.psum((node_local, edge_local), ("dp", "group"))
    weights = jnp.where(node_live, total_node / (node_float * all_nodes), 0.0)
    coefs = coefficients(used, node_counts, edge_counts, total_node, total_edge)
    matrix = coef_matrix(neighbors, coefs)
    input_b, pair_b, proj_b, head_b = (
        lax.all_gather(input_weight.astype(jnp.bfloat16), ("dp", "group"), axis=1, tiled=True),
        lax.all_gather(pair_weight.astype(jnp.bfloat16), ("dp", "group"), axis=2, tiled=True),
        lax.all_gather(proj_weight.astype(jnp.bfloat16), ("dp", "group"), axis=1, tiled=True),
        lax.all_gather(head_weight.astype(jnp.bfloat16), ("dp", "group"), axis=0, tiled=True),
    )
    hidden = jnp.dot(features, input_b, preferred_element_type=jnp.float32).astype(jnp.bfloat16)
    kept = []
    for layer_index in range(LAYERS):
        hidden, saved = layer_forward(hidden, pair_b[layer_index], proj_b[layer_index], matrix)
        kept.append(saved)
    logits = jnp.dot(hidden, head_b, preferred_element_type=jnp.float32)
    log_total = jax.nn.logsumexp(logits, axis=1)
    targets = (labels[:, None] == lax.iota(jnp.int32, logits.shape[1])[None, :]).astype(jnp.float32)
    loss_local = jnp.sum(weights * (log_total - jnp.sum(logits * targets, axis=1)))
    loss_sum, weight_sum = lax.psum((loss_local, jnp.sum(weights)), ("dp", "group"))
    grad_logits = (
        (weights / weight_sum)[:, None] * (jnp.exp(logits - log_total[:, None]) - targets)
    ).astype(jnp.bfloat16)
    grad_head = contract_rows(hidden, grad_logits)
    grad_hidden = contract_cols(grad_logits, head_b)
    pair_grads = [None] * LAYERS
    proj_grads = [None] * LAYERS
    for layer_index in reversed(range(LAYERS)):
        grad_hidden, grad_pair, grad_proj = layer_backward(
            grad_hidden, kept[layer_index], pair_b[layer_index], proj_b[layer_index], matrix
        )
        pair_grads[layer_index] = grad_pair
        proj_grads[layer_index] = grad_proj
    grad_input = contract_rows(features, grad_hidden.astype(jnp.bfloat16))
    grad_input, grad_pairs, grad_projs, grad_head = (
        lax.psum_scatter(grad_input, ("dp", "group"), scatter_dimension=1, tiled=True),
        lax.psum_scatter(jnp.stack(pair_grads), ("dp", "group"), scatter_dimension=2, tiled=True),
        lax.psum_scatter(jnp.stack(proj_grads), ("dp", "group"), scatter_dimension=1, tiled=True),
        lax.psum_scatter(grad_head, ("dp", "group"), scatter_dimension=0, tiled=True),
    )
    input_new, input_first_new, input_second_new = adamw_update(
        input_weight, input_first, input_second, grad_input
    )
    pair_new, pair_first_new, pair_second_new = adamw_update(
        pair_weight, pair_first, pair_second, grad_pairs
    )
    proj_new, proj_first_new, proj_second_new = adamw_update(
        proj_weight, proj_first, proj_second, grad_projs
    )
    head_new, head_first_new, head_second_new = adamw_update(
        head_weight, head_first, head_second, grad_head
    )
    return (
        loss_sum / weight_sum,
        weight_sum / all_nodes,
        input_new,
        pair_new,
        proj_new,
        head_new,
        input_first_new,
        pair_first_new,
        proj_first_new,
        head_first_new,
        input_second_new,
        pair_second_new,
        proj_second_new,
        head_second_new,
        input_new.astype(jnp.bfloat16),
        pair_new.astype(jnp.bfloat16),
        proj_new.astype(jnp.bfloat16),
        head_new.astype(jnp.bfloat16),
    )


def solution(mesh):
    placed = (
        P(("dp", "group"), None),
        P(("dp", "group")),
        P(("dp", "group"), None),
        P(("dp", "group")),
        P(("dp", "group")),
        P(("dp", "group"), None),
        P(("dp", "group")),
        P(None, ("dp", "group")),
        P(None, None, ("dp", "group")),
        P(None, ("dp", "group"), None),
        P(("dp", "group"), None),
        P(None, ("dp", "group")),
        P(None, None, ("dp", "group")),
        P(None, ("dp", "group"), None),
        P(("dp", "group"), None),
        P(None, ("dp", "group")),
        P(None, None, ("dp", "group")),
        P(None, ("dp", "group"), None),
        P(("dp", "group"), None),
    )
    return jax.shard_map(
        body,
        mesh=mesh,
        in_specs=placed,
        out_specs=(
            P(),
            P(),
            P(None, ("dp", "group")),
            P(None, None, ("dp", "group")),
            P(None, ("dp", "group"), None),
            P(("dp", "group"), None),
            P(None, ("dp", "group")),
            P(None, None, ("dp", "group")),
            P(None, ("dp", "group"), None),
            P(("dp", "group"), None),
            P(None, ("dp", "group")),
            P(None, None, ("dp", "group")),
            P(None, ("dp", "group"), None),
            P(("dp", "group"), None),
            P(None, ("dp", "group")),
            P(None, None, ("dp", "group")),
            P(None, ("dp", "group"), None),
            P(("dp", "group"), None),
        ),
        check_vma=False,
    )
```

profile of v0, /device:TPU:0, one launch (start us, length us, event | category | flops | bytes accessed | tf_op | source)
XLA Modules:
  0.0 968.3 jit_solution(10317203372323273497)
XLA Ops:
  15.6 42.2 %all-reduce.1 = (f32[]{:T(128)}, f32[]{:T(128)}) all-reduce(f32[]{:T(128)} %select_reduce_fusion.2, f32[]{:T(128)} %get-tuple-element.56), channel_id=1, replica_groups=mesh['dp'=8,'group'=4] {'dp','group'}, use_global_device_ids=true, to_apply=%region_1.2 | all-reduce | flops 2 | bytes 16 | tf_op jit(solution)/shard_map/psum | solution.py:146
  60.8 19.7 %select_add_fusion.15 = f32[2048,2048]{1,0:T(8,128)} fusion(f32[2048]{0:T(1024)S(1)} %bitcast.162, s32[2048]{0:T(1024)S(1)} %bitcast.144, f32[2048]{0:T(1024)S(1)} %bitcast.168, s32[2048]{0:T(1024)S(1)} %bitcast.150, f32[2048]{0:T(1024)S(1)} %bitcast.174, s32[2048]{0:T(1024)S(1)} %bitcast.114, f32[2048]{0:T(1024)S(1)} %bitcast.180, ...), kind=kLoop, calls=%fused_computation.clone.2.clone | loop fusion | flops 96468992 | bytes 16908288 | tf_op jit(solution)/shard_map/dot_general | solution.py:98
  80.5 19.5 %select_add_fusion.14 = f32[2048,2048]{1,0:T(8,128)} fusion(f32[2048]{0:T(1024)S(1)} %bitcast.163, s32[2048]{0:T(1024)S(1)} %bitcast.145, f32[2048]{0:T(1024)S(1)} %bitcast.169, s32[2048]{0:T(1024)S(1)} %bitcast.151, f32[2048]{0:T(1024)S(1)} %bitcast.175, s32[2048]{0:T(1024)S(1)} %bitcast.115, f32[2048]{0:T(1024)S(1)} %bitcast.181, ...), kind=kLoop, calls=%fused_computation.clone.1.clone.1 | loop fusion | flops 96468992 | bytes 16908288 | tf_op jit(solution)/shard_map/dot_general | solution.py:98
  100.0 19.6 %select_add_fusion.13 = f32[2048,2048]{1,0:T(8,128)} fusion(f32[2048]{0:T(1024)S(1)} %bitcast.164, s32[2048]{0:T(1024)S(1)} %bitcast.146, f32[2048]{0:T(1024)S(1)} %bitcast.170, s32[2048]{0:T(1024)S(1)} %bitcast.152, f32[2048]{0:T(1024)S(1)} %bitcast.176, s32[2048]{0:T(1024)S(1)} %bitcast.116, f32[2048]{0:T(1024)S(1)} %bitcast.182, ...), kind=kLoop, calls=%fused_computation.clone.clone.1 | loop fusion | flops 96468992 | bytes 16908288 | tf_op jit(solution)/shard_map/dot_general | solution.py:98
  119.7 43.6 %all_gather.15 = bf16[512,41]{1,0:T(8,128)(2,1)} all-gather(bf16[16,41]{1,0:T(8,128)(2,1)S(1)} %convert_element_type.102), channel_id=1, replica_groups=mesh['dp'=8,'group'=4] {'dp','group'}, dimensions={0}, use_global_device_ids=true | all-gather | bytes 43296 | tf_op jit(solution)/shard_map/all_gather | solution.py:154
  163.3 38.5 %all_gather.12 = bf16[602,512]{0,1:T(8,128)(2,1)S(1)} all-gather(bf16[602,16]{0,1:T(8,128)(2,1)S(1)} %convert_element_type.90), channel_id=1, replica_groups=mesh['dp'=8,'group'=4] {'dp','group'}, dimensions={1}, use_global_device_ids=true | all-gather | bytes 635712 | tf_op jit(solution)/shard_map/all_gather | solution.py:151
  205.1 30.5 %convolution_convert_fusion.12 = bf16[2048,512]{1,0:T(8,128)(2,1)} fusion(bf16[2048,512]{1,0:T(8,128)(2,1)S(1)} %convolution_convert_fusion.9, f32[2048]{0:T(1024)S(1)} %bitcast.165, s32[2048]{0:T(1024)S(1)} %bitcast.147, f32[2048]{0:T(1024)S(1)} %bitcast.171, s32[2048]{0:T(1024)S(1)} %bitcast.153, f32[2048]{0:T(1024)S(1)} %bitcast.177, ...), kind=kOutput, calls=%fused_computation.71 | convolution fusion | flops 25867321344 | bytes 4325376 | tf_op jit(solution)/shard_map/dot_general | solution.py:69
  244.2 5.5 multiply_reduce_fusion.5
  253.2 29.4 %convolution_convert_fusion.11 = bf16[2048,512]{1,0:T(8,128)(2,1)S(1)} fusion(bf16[2048,512]{0,1:T(8,128)(2,1)S(1)} %multiply_convert_fusion.2, f32[2048]{0:T(1024)S(1)} %bitcast.166, s32[2048]{0:T(1024)S(1)} %bitcast.148, f32[2048]{0:T(1024)S(1)} %bitcast.172, s32[2048]{0:T(1024)S(1)} %bitcast.154, f32[2048]{0:T(1024)S(1)} %bitcast.178, ...), kind=kOutput, calls=%fused_computation.70 | convolution fusion | flops 25867321344 | bytes 4325376 | tf_op jit(solution)/shard_map/dot_general | solution.py:69
  286.6 3.7 multiply_reduce_fusion.4
  293.9 29.7 %convolution_convert_fusion.10 = bf16[2048,512]{1,0:T(8,128)(2,1)S(1)} fusion(bf16[2048,512]{0,1:T(8,128)(2,1)S(1)} %multiply_convert_fusion.1, f32[2048]{0:T(1024)S(1)} %bitcast.167, s32[2048]{0:T(1024)S(1)} %bitcast.149, f32[2048]{0:T(1024)S(1)} %bitcast.173, s32[2048]{0:T(1024)S(1)} %bitcast.155, f32[2048]{0:T(1024)S(1)} %bitcast.179, ...), kind=kOutput, calls=%fused_computation.69 | convolution fusion | flops 25867321344 | bytes 4325376 | tf_op jit(solution)/shard_map/dot_general | solution.py:69
  326.2 3.7 multiply_reduce_fusion.3
  335.1 37.2 %all-reduce = (f32[]{:T(128)}, f32[]{:T(128)}) all-reduce(f32[]{:T(128)} %get-tuple-element.59, f32[]{:T(128)} %get-tuple-element.58), channel_id=1, replica_groups=mesh['dp'=8,'group'=4] {'dp','group'}, use_global_device_ids=true, to_apply=%region_12.13 | all-reduce | flops 2 | bytes 16 | tf_op jit(solution)/shard_map/psum | solution.py:165
  374.2 4.7 fusion.53
  378.9 6.6 multiply_reduce_fusion.2
  386.3 5.9 fusion.20
  393.5 3.8 convolution_convert_fusion.2
  401.1 29.2 %fusion.87 = f32[2048,512]{0,1:T(8,128)} fusion(f32[2048,512]{1,0:T(8,128)S(1)} %fusion.43, f32[2048,2048]{1,0:T(8,128)S(1)} %bitcast.106), kind=kOutput, calls=%fused_computation.180 | convolution fusion | flops 25769803776 | bytes 25165824 | tf_op jit(solution)/shard_map/dot_general | solution.py:98
  430.3 4.3 multiply_reduce_fusion.1
  434.7 3.5 fusion.13
  438.2 4.4 convolution_convert_fusion.1
  446.4 29.2 %fusion.86 = f32[2048,512]{0,1:T(8,128)} fusion(f32[2048,512]{1,0:T(8,128)S(1)} %fusion.36, f32[2048,2048]{1,0:T(8,128)S(1)} %bitcast.104), kind=kOutput, calls=%fused_computation.179 | convolution fusion | flops 25769803776 | bytes 25165824 | tf_op jit(solution)/shard_map/dot_general | solution.py:98
  475.6 4.2 multiply_reduce_fusion
  479.9 3.5 fusion.6
  484.7 3.8 convolution_convert_fusion
  492.7 28.5 %fusion.85 = f32[2048,512]{1,0:T(8,128)} fusion(f32[2048,512]{1,0:T(8,128)S(1)} %fusion.29, f32[2048,2048]{1,0:T(8,128)S(1)} %bitcast.102), kind=kOutput, calls=%fused_computation.178 | convolution fusion | flops 25769803776 | bytes 25165824 | tf_op jit(solution)/shard_map/dot_general | solution.py:98
  521.2 6.4 convolution_bitcast_fusion
  534.0 3.7 fusion.27
  549.6 5.4 fusion.50
  567.2 104.0 %reduce-scatter.13.cloned.1.call-done = f32[16,602]{1,0:T(8,128)} async-done(((f32[512,602]{1,0:T(8,128)}), f32[16,602]{1,0:T(8,128)}) %reduce-scatter.13.cloned.1.call-update) | async-done | bytes 38544
  672.7 141.4 %reduce-scatter.7.cloned.1.call-done = f32[3,512,32]{1,2,0:T(8,128)} async-done(((f32[3,512,1024]{1,2,0:T(8,128)}), f32[3,512,32]{1,2,0:T(8,128)}) %reduce-scatter.7.cloned.1.call-update) | async-done | bytes 196624 | tf_op jit(solution)/shard_map/reduce_scatter | solution.py:182
  815.9 141.1 %reduce-scatter.9.cloned.1.call-done = f32[3,32,512]{2,1,0:T(8,128)} async-done(((f32[3,1024,512]{2,1,0:T(8,128)}), f32[3,32,512]{2,1,0:T(8,128)}) %reduce-scatter.9.cloned.1.call-update) | async-done | bytes 196624 | tf_op jit(solution)/shard_map/reduce_scatter | solution.py:183
  (278 shorter events, 91.2 us)
Async XLA Ops:
  7.2 194.6 %copy-start = (bf16[2048,602]{0,1:T(8,128)(2,1)S(1)}, bf16[2048,602]{0,1:T(8,128)(2,1)}, u32[]{:S(2)}) copy-start(bf16[2048,602]{0,1:T(8,128)(2,1)} %param.19) | copy-start | bytes 7397380
  7.2 228.4 %all-gather.3.cloned.1.call-start = ((), (), s32[]{:S(2)}) async-start(), calls=%async_computation.4 | async-start | bytes 3244032 | tf_op jit(solution)/shard_map/all_gather | solution.py:152
  9.0 235.2 %all-gather.5.cloned.1.call-start = ((), (), s32[]{:S(2)}) async-start(), calls=%async_computation.5 | async-start | bytes 3244032 | tf_op jit(solution)/shard_map/all_gather | solution.py:153
  10.7 555.2 %reduce-scatter.11.cloned.1.call-start = ((), (), s32[]{:S(2)}) async-start(), calls=%async_computation.8 | async-start | bytes 270336 | tf_op jit(solution)/shard_map/reduce_scatter | solution.py:184
  12.7 191.0 %copy-start.32 = (s32[2048,1]{0,1:T(1,128)}, s32[2048,1]{0,1:T(1,128)S(1)}, u32[]{:S(2)}) copy-start(s32[2048,1]{0,1:T(1,128)S(1)} %get-tuple-element.87) | copy-start | bytes 24580
  12.7 191.0 %copy-start.34 = (s32[2048,1]{0,1:T(1,128)}, s32[2048,1]{0,1:T(1,128)S(1)}, u32[]{:S(2)}) copy-start(s32[2048,1]{0,1:T(1,128)S(1)} %get-tuple-element.88) | copy-start | bytes 24580
  12.7 191.0 %copy-start.36 = (s32[2048,1]{0,1:T(1,128)}, s32[2048,1]{0,1:T(1,128)S(1)}, u32[]{:S(2)}) copy-start(s32[2048,1]{0,1:T(1,128)S(1)} %get-tuple-element.89) | copy-start | bytes 24580
  12.7 191.0 %copy-start.38 = (s32[2048,1]{0,1:T(1,128)}, s32[2048,1]{0,1:T(1,128)S(1)}, u32[]{:S(2)}) copy-start(s32[2048,1]{0,1:T(1,128)S(1)} %get-tuple-element.90) | copy-start | bytes 24580
  12.7 191.0 %copy-start.40 = (s32[2048,1]{0,1:T(1,128)}, s32[2048,1]{0,1:T(1,128)S(1)}, u32[]{:S(2)}) copy-start(s32[2048,1]{0,1:T(1,128)S(1)} %get-tuple-element.91) | copy-start | bytes 24580
  12.7 191.0 %copy-start.42 = (s32[2048,1]{0,1:T(1,128)}, s32[2048,1]{0,1:T(1,128)S(1)}, u32[]{:S(2)}) copy-start(s32[2048,1]{0,1:T(1,128)S(1)} %get-tuple-element.92) | copy-start | bytes 24580
  60.7 143.0 %copy-start.44 = (f32[2048,1]{0,1:T(1,128)}, f32[2048,1]{0,1:T(1,128)S(1)}, u32[]{:S(2)}) copy-start(f32[2048,1]{0,1:T(1,128)S(1)} %get-tuple-element.93) | copy-start | bytes 24580
  60.7 143.0 %copy-start.46 = (f32[2048,1]{0,1:T(1,128)}, f32[2048,1]{0,1:T(1,128)S(1)}, u32[]{:S(2)}) copy-start(f32[2048,1]{0,1:T(1,128)S(1)} %get-tuple-element.94) | copy-start | bytes 24580
  60.8 143.0 %copy-start.48 = (f32[2048,1]{0,1:T(1,128)}, f32[2048,1]{0,1:T(1,128)S(1)}, u32[]{:S(2)}) copy-start(f32[2048,1]{0,1:T(1,128)S(1)} %get-tuple-element.95) | copy-start | bytes 24580
  60.8 143.0 %copy-start.50 = (f32[2048,1]{0,1:T(1,128)}, f32[2048,1]{0,1:T(1,128)S(1)}, u32[]{:S(2)}) copy-start(f32[2048,1]{0,1:T(1,128)S(1)} %get-tuple-element.96) | copy-start | bytes 24580
  60.8 143.0 %copy-start.52 = (f32[2048,1]{0,1:T(1,128)}, f32[2048,1]{0,1:T(1,128)S(1)}, u32[]{:S(2)}) copy-start(f32[2048,1]{0,1:T(1,128)S(1)} %get-tuple-element.97) | copy-start | bytes 24580
  60.8 143.0 %copy-start.54 = (f32[2048,1]{0,1:T(1,128)}, f32[2048,1]{0,1:T(1,128)S(1)}, u32[]{:S(2)}) copy-start(f32[2048,1]{0,1:T(1,128)S(1)} %get-tuple-element.98) | copy-start | bytes 24580
  60.8 143.0 %copy-start.56 = (f32[2048,1]{0,1:T(1,128)}, f32[2048,1]{0,1:T(1,128)S(1)}, u32[]{:S(2)}) copy-start(f32[2048,1]{0,1:T(1,128)S(1)} %get-tuple-element.99) | copy-start | bytes 24580
  60.8 143.0 %copy-start.58 = (f32[2048,1]{0,1:T(1,128)}, f32[2048,1]{0,1:T(1,128)S(1)}, u32[]{:S(2)}) copy-start(f32[2048,1]{0,1:T(1,128)S(1)} %get-tuple-element.100) | copy-start | bytes 24580
  249.6 33.0 %copy-start.68 = (f32[2048]{0:T(1024)}, f32[2048]{0:T(1024)S(1)}, u32[]{:S(2)}) copy-start(f32[2048]{0:T(1024)S(1)} %get-tuple-element.101) | copy-start | bytes 24580
  249.8 32.8 %copy-start.62 = (f32[2048]{0:T(1024)}, f32[2048]{0:T(1024)S(1)}, u32[]{:S(2)}) copy-start(f32[2048]{0:T(1024)S(1)} %fusion.74) | copy-start | bytes 24580
  385.5 285.7 %reduce-scatter.13.cloned.1.call-start = ((), (), s32[]{:S(2)}) async-start(), calls=%async_computation.9 | async-start | bytes 1351680
  397.3 32.9 %copy-start.6 = (bf16[2048,1024]{1,0:T(8,128)(2,1)}, bf16[2048,1024]{1,0:T(8,128)(2,1)S(1)}, u32[]{:S(2)}) copy-start(bf16[2048,1024]{1,0:T(8,128)(2,1)S(1)} %convolution_convert_fusion.2) | copy-start | bytes 12582916
  442.7 32.9 %copy-start.8 = (bf16[2048,1024]{1,0:T(8,128)(2,1)}, bf16[2048,1024]{1,0:T(8,128)(2,1)S(1)}, u32[]{:S(2)}) copy-start(bf16[2048,1024]{1,0:T(8,128)(2,1)S(1)} %convolution_convert_fusion.1) | copy-start | bytes 12582916
  534.0 280.1 %reduce-scatter.7.cloned.1.call-start = ((), (), s32[]{:S(2)}) async-start(), calls=%async_computation.6 | async-start | bytes 6488064 | tf_op jit(solution)/shard_map/reduce_scatter | solution.py:182
  549.3 407.7 %reduce-scatter.9.cloned.1.call-start = ((), (), s32[]{:S(2)}) async-start(), calls=%async_computation.7 | async-start | bytes 6488064 | tf_op jit(solution)/shard_map/reduce_scatter | solution.py:183
  563.7 107.6 %copy-start.31 = (f32[602,16]{0,1:T(8,128)S(1)}, f32[602,16]{0,1:T(8,128)}, u32[]{:S(2)}) copy-start(f32[602,16]{0,1:T(8,128)} %param.26) | copy-start | bytes 115588
  563.7 107.6 %copy-start.66 = (f32[602,16]{0,1:T(8,128)S(1)}, f32[602,16]{0,1:T(8,128)}, u32[]{:S(2)}) copy-start(f32[602,16]{0,1:T(8,128)} %param.30) | copy-start | bytes 115588
  563.7 250.4 %copy-start.24 = (f32[3,512,32]{1,2,0:T(8,128)S(1)}, f32[3,512,32]{1,2,0:T(8,128)}, u32[]{:S(2)}) copy-start(f32[3,512,32]{1,2,0:T(8,128)} %param.27) | copy-start | bytes 589828
  563.7 250.4 %copy-start.27 = (f32[3,512,32]{1,2,0:T(8,128)S(1)}, f32[3,512,32]{1,2,0:T(8,128)}, u32[]{:S(2)}) copy-start(f32[3,512,32]{1,2,0:T(8,128)} %param.31) | copy-start | bytes 589828
  563.7 250.4 %copy-start.28 = (f32[3,512,32]{1,2,0:T(8,128)S(1)}, f32[3,512,32]{1,2,0:T(8,128)}, u32[]{:S(2)}) copy-start(f32[3,512,32]{1,2,0:T(8,128)} %param.35) | copy-start | bytes 589828
  563.7 393.4 %copy-start.25 = (f32[3,32,512]{2,1,0:T(8,128)S(1)}, f32[3,32,512]{2,1,0:T(8,128)}, u32[]{:S(2)}) copy-start(f32[3,32,512]{2,1,0:T(8,128)} %param.28) | copy-start | bytes 589828
  563.7 393.3 %copy-start.29 = (f32[3,32,512]{2,1,0:T(8,128)S(1)}, f32[3,32,512]{2,1,0:T(8,128)}, u32[]{:S(2)}) copy-start(f32[3,32,512]{2,1,0:T(8,128)} %param.32) | copy-start | bytes 589828
  (78 other events, 458.8 us)
Sparse Core Ops, SparseCore 0:
  11.5 62.2 all-gather.2
  77.3 58.6 all-gather.4
  385.7 135.4 reduce-scatter.10
  534.1 137.1 reduce-scatter.12
  673.4 140.6 reduce-scatter.6
  816.2 140.7 reduce-scatter.8
where the time goes:
time: 975 us; the launch traced here: 968 us
  waiting for transfers between devices  387 us (40%)
  matrix products  268 us (27%)
  blocking collectives  162 us (17%)
  other arithmetic  102 us (10%)
  local copies, waits for them, and re-layouts  29.4 us (3%)
  between operations  20.8 us (2%)
    reduce_scatter x1, waiting for transfers between devices, body(): lax.psum_scatter(jnp.stack(pair_grads), ('dp', 'group'), scatter_dimensio...  141 us
    reduce_scatter x1, waiting for transfers between devices, body(): lax.psum_scatter(jnp.stack(proj_grads), ('dp', 'group'), scatter_dimensio...  141 us
    unnamed x7, waiting for transfers between devices  104 us
    dot_general x3, matrix products, layer_forward(): jnp.dot(matrix, hidden.astype(jnp.float32), precision=lax.Precision.HIGHE...  89.6 us
    dot_general x3, matrix products, layer_backward(): lax.dot_general(matrix, grad_pooled, (((0,), (0,)), ((), ())), precision=...  86.8 us
    dot_general x3, other arithmetic, layer_backward(): lax.dot_general(matrix, grad_pooled, (((0,), (0,)), ((), ())), precision=...  58.8 us
    all_gather x1, blocking collectives, body(): lax.all_gather(head_weight.astype(jnp.bfloat16), ('dp', 'group'), axis=0,...  43.6 us
    psum x1, blocking collectives, body(): total_node, total_edge = lax.psum((node_local, edge_local), ('dp', 'group'))  42.2 us
  transfers between devices with their start and end apart: 6, of which 3 were waited for; matrix products, arithmetic and copies ran while one was open for 29% of the time, Pallas kernels for 0%

commit v1 on v0

--- a/solution.py
+++ b/solution.py
@@ -1,11 +1,13 @@
 import jax
 import jax.numpy as jnp
 from jax import lax
+from jax.experimental import pallas as pl
+from jax.experimental.pallas import tpu as pltpu
 from jax.sharding import PartitionSpec as P
 
 LAYERS = 3
 STEP = 5
-
+COMMON = 840.0
 
 learn_rate = 0.03
 beta_first = 0.5
@@ -13,6 +15,685 @@
 adam_eps = 1e-08
 decay_rate = 0.01
 norm_eps = 1e-06
+
+AXES = ("dp", "group")
+MESH = pl.DeviceIdType.MESH
+f32 = jnp.float32
+bf16 = jnp.bfloat16
+TILE = 512
+ROWS = 64
+GELU_IN = 0.7978845608028654
+GELU_CUBE = 0.044715
+
+
+def dot_nn(left, right):
+    return jnp.dot(left, right, preferred_element_type=f32)
+
+
+def dot_nt(left, right):
+    return lax.dot_general(left, right, (((1,), (1,)), ((), ())), preferred_element_type=f32)
+
+
+def adamw_update(weight, first, second, grad):
+    first_new = beta_first * first + (1.0 - beta_first) * grad
+    second_new = beta_second * second + (1.0 - beta_second) * grad * grad
+    first_hat = first_new / (1.0 - beta_first**STEP)
+    second_hat = second_new / (1.0 - beta_second**STEP)
+    weight_new = weight - learn_rate * (
+        first_hat / (jnp.sqrt(second_hat) + adam_eps) + decay_rate * weight
+    )
+    return (weight_new, first_new, second_new)
+
+
+class Place:
+    def __init__(self):
+        dp, group = lax.axis_index("dp"), lax.axis_index("group")
+        self.z, self.y = dp // 2, dp % 2
+        self.x, self.c = group // 2, group % 2
+        self.far_y, self.far_x, self.far_c = 1 - self.y, 1 - self.x, 1 - self.c
+        self.sibling = (dp, group + 1 - 2 * self.c)
+        self.beside_x = (dp, group + 2 - 4 * self.x)
+        self.beside_y = (dp + 1 - 2 * self.y, group)
+        self.later_z = [(self.z + step) % 4 for step in (1, 2, 3)]
+        self.earlier_z = [(self.z + 4 - step) % 4 for step in (1, 2, 3)]
+        self.to_z = [(at * 2 + self.y, group) for at in self.later_z]
+        self.from_z = [(at * 2 + self.y, group) for at in self.earlier_z]
+
+    def partners(self):
+        return [self.sibling, self.beside_x, self.beside_y] + self.to_z
+
+
+class Wire:
+    def __init__(self, send_sems, recv_sems):
+        self.send_sems, self.recv_sems = send_sems, recv_sems
+        self.sent = []
+
+    def copy(self, at, source, target, device):
+        return pltpu.make_async_remote_copy(
+            src_ref=source(),
+            dst_ref=target(),
+            send_sem=self.send_sems.at[at],
+            recv_sem=self.recv_sems.at[at],
+            device_id=device,
+            device_id_type=MESH,
+        )
+
+    def send(self, at, source, target, device):
+        self.copy(at, source, target, device).start()
+        self.sent.append((at, source, target, device))
+
+    def arrived(self, at, target, device):
+        self.copy(at, target, target, device).wait_recv()
+
+    def finish(self):
+        for sent in self.sent:
+            self.copy(*sent).wait_send()
+        self.sent = []
+
+
+def gather_steps(place, wire, region):
+    z, y, x, c = place.z, place.y, place.x, place.c
+    fy, fx, fc = place.far_y, place.far_x, place.far_c
+    whole, low, high = slice(0, 4), slice(0, 2), slice(2, 4)
+
+    def at(*index):
+        return lambda: region(*index)
+
+    def send(sem, index, device):
+        wire.send(sem, at(*index), at(*index), device)
+
+    for step in range(3):
+        send(step, (z, y, x, c), place.to_z[step])
+    yield
+    for step in range(3):
+        wire.arrived(step, at(place.earlier_z[step], y, x, c), place.from_z[step])
+    send(3, (whole, y, x, c), place.beside_x)
+    send(4, (whole, y, x, c), place.beside_y)
+    send(5, (whole, y, x, c), place.sibling)
+    yield
+    wire.arrived(3, at(whole, y, fx, c), place.beside_x)
+    send(6, (low, y, fx, c), place.beside_y)
+    send(8, (whole, y, fx, c), place.sibling)
+    wire.arrived(4, at(whole, fy, x, c), place.beside_y)
+    send(7, (high, fy, x, c), place.beside_x)
+    send(9, (whole, fy, x, c), place.sibling)
+    yield
+    wire.arrived(6, at(low, fy, fx, c), place.beside_y)
+    wire.arrived(7, at(high, fy, fx, c), place.beside_x)
+    send(10, (whole, fy, fx, c), place.sibling)
+    yield
+    wire.arrived(5, at(whole, y, x, fc), place.sibling)
+    wire.arrived(8, at(whole, y, fx, fc), place.sibling)
+    wire.arrived(9, at(whole, fy, x, fc), place.sibling)
+    wire.arrived(10, at(whole, fy, fx, fc), place.sibling)
+    yield
+
+
+def scatter_steps(place, wire, bufs, slot, store):
+    grads, from_core, out_half, in_half, out_col, in_col, out_z, in_z = bufs
+    z, y, x, c = place.z, place.y, place.x, place.c
+    fy, fx, fc = place.far_y, place.far_x, place.far_c
+    low, high = slice(0, 2), slice(2, 4)
+
+    def at(buf, *index):
+        return lambda: buf.at[(slot, *index)]
+
+    def both(zs, yy, xx):
+        return grads[slot, zs, yy, xx, c].astype(f32) + from_core[slot, zs, yy, xx].astype(f32)
+
+    wire.send(0, at(grads, slice(0, 4), slice(0, 2), slice(0, 2), fc), at(from_core), place.sibling)
+    yield
+    wire.arrived(0, at(from_core), place.sibling)
+    out_half[slot, 0] = both(low, fy, fx).astype(bf16)
+    wire.send(1, at(out_half, 0), at(in_half, 0), place.beside_x)
+    out_half[slot, 1] = both(high, fy, fx).astype(bf16)
+    wire.send(2, at(out_half, 1), at(in_half, 1), place.beside_y)
+    yield
+    wire.arrived(1, at(in_half, 0), place.beside_x)
+    out_col[slot, 1, low] = (both(low, fy, x) + in_half[slot, 0].astype(f32)).astype(bf16)
+    out_col[slot, 1, high] = both(high, fy, x).astype(bf16)
+    wire.send(4, at(out_col, 1), at(in_col, 1), place.beside_y)
+    wire.arrived(2, at(in_half, 1), place.beside_y)
+    out_col[slot, 0, low] = both(low, y, fx).astype(bf16)
+    out_col[slot, 0, high] = (both(high, y, fx) + in_half[slot, 1].astype(f32)).astype(bf16)
+    wire.send(3, at(out_col, 0), at(in_col, 0), place.beside_x)
+    yield
+    wire.arrived(3, at(in_col, 0), place.beside_x)
+    wire.arrived(4, at(in_col, 1), place.beside_y)
+
+    def column(zz):
+        beside = in_col[slot, 0, zz].astype(f32) + in_col[slot, 1, zz].astype(f32)
+        return both(zz, y, x) + beside
+
+    for step in range(3):
+        out_z[slot, step] = column(place.later_z[step]).astype(bf16)
+        wire.send(5 + step, at(out_z, step), at(in_z, step), place.to_z[step])
+    yield
+    for step in range(3):
+        wire.arrived(5 + step, at(in_z, step), place.from_z[step])
+    others = in_z[slot, 0].astype(f32) + in_z[slot, 1].astype(f32) + in_z[slot, 2].astype(f32)
+    store(column(z) + others)
+    wire.finish()
+    yield
+
+
+def sum_steps(place, wire, bufs, slot, store):
+    out, arrive, line = bufs
+
+    def at(buf, *index):
+        return lambda: buf.at[(slot, *index)]
+
+    for stage, device in enumerate((place.sibling, place.beside_x, place.beside_y)):
+        wire.send(stage, at(out, stage), at(arrive, stage), device)
+        yield
+        wire.arrived(stage, at(arrive, stage), device)
+        if stage < 2:
+            out[slot, stage + 1] = out[slot, stage] + arrive[slot, stage]
+        else:
+            line[slot, place.z] = out[slot, stage] + arrive[slot, stage]
+    for step in range(3):
+        wire.send(3 + step, at(line, place.z), at(line, place.z), place.to_z[step])
+    yield
+    for step in range(3):
+        wire.arrived(3 + step, at(line, place.earlier_z[step]), place.from_z[step])
+    store((line[slot, 0] + line[slot, 1]) + (line[slot, 2] + line[slot, 3]))
+    wire.finish()
+    yield
+
+
+def step(*generators):
+    for generator in generators:
+        next(generator)
+
+
+def row_of_scalars(values):
+    rows = lax.broadcasted_iota(jnp.int32, (8, 128), 0)
+    block = jnp.zeros((8, 128), f32)
+    for at, value in enumerate(values):
+        block = jnp.where(rows == at, value, block)
+    return block
+
+
+def gelu(pre):
+    bend = jnp.tanh(GELU_IN * (pre + GELU_CUBE * (pre * pre * pre)))
+    return 0.5 * pre * (1.0 + bend), bend
+
+
+def lane_chunks(tile):
+    for at in range(0, TILE, 128):
+        yield pl.ds(tile + at, 128), slice(at, at + 128)
+
+
+def row_chunks():
+    return [slice(at, at + ROWS) for at in range(0, 512, ROWS)]
+
+
+def norm_forward(pre, active, out, at_pre, at_out):
+    for (lanes, _), (to_lanes, _) in zip(lane_chunks(at_pre), lane_chunks(at_out)):
+        square = jnp.zeros((ROWS, 128), f32)
+        for row in row_chunks():
+            value, _ = gelu(pre[row, lanes])
+            active[row, :] = value
+            square = square + value * value
+        square = jnp.sum(square, axis=0, keepdims=True)
+        scale = lax.rsqrt(square * (1.0 / 512) + norm_eps)
+        for row in row_chunks():
+            out[row, to_lanes] = (active[row, :] * scale).astype(bf16)
+
+
+def norm_backward(grad, pre, active, slope, out, at_pre, at_out):
+    for (lanes, inside), (to_lanes, _) in zip(lane_chunks(at_pre), lane_chunks(at_out)):
+        square = jnp.zeros((ROWS, 128), f32)
+        along = jnp.zeros((ROWS, 128), f32)
+        for row in row_chunks():
+            at = pre[row, lanes]
+            value, bend = gelu(at)
+            active[row, :] = value
+            slope[row, :] = 0.5 * (1.0 + bend) + (0.5 * GELU_IN) * at * (1.0 - bend * bend) * (
+                1.0 + (3.0 * GELU_CUBE) * (at * at)
+            )
+            square = square + value * value
+            along = along + value * grad[row, inside]
+        square = jnp.sum(square, axis=0, keepdims=True)
+        along = jnp.sum(along, axis=0, keepdims=True) * (1.0 / 512)
+        scale = lax.rsqrt(square * (1.0 / 512) + norm_eps)
+        pull = scale * scale * scale * along
+        for row in row_chunks():
+            out[row, to_lanes] = (
+                slope[row, :] * (scale * grad[row, inside] - active[row, :] * pull)
+            ).astype(bf16)
+
+
+def ticks(at, plan):
+    for when, generators in plan.items():
+
+        @pl.when(at == when)
+        def _(generators=generators):
+            step(*generators)
+
+
+def train_kernel(
+    feat_hbm, nbr, edge, degree, counts, labels, live, win_own, pair_own, proj_own, head_own,
+    gin_out, gpair_out, gproj_out, ghead_out, scal_out,
+    matrix, feat, hid_0, hid_1, hid_2, pool_0, pool_1, pool_2, join_0, join_1, join_2, pre_0, pre_1,
+    win, weights, head, turned, head_grad, scale, inverse, terms, totals, losses,
+    back, top_pre, last, active, slope,
+    big_g, big_rc, big_oh, big_ih, big_ocol, big_icol, big_oz, big_iz,
+    in_g, in_rc, in_oh, in_ih, in_ocol, in_icol, in_oz, in_iz,
+    hd_g, hd_rc, hd_oh, hd_ih, hd_ocol, hd_icol, hd_oz, hd_iz,
+    sum_out, sum_in, sum_line,
+    gather_send, gather_recv, scatter_send, scatter_recv, sum_send, sum_recv, feat_sem,
+):
+    place = Place()
+    z, y, x, c = place.z, place.y, place.x, place.c
+    nodes, width, classes = nbr.shape[1], hid_0.shape[0], head_own.shape[1]
+    steps = nodes // TILE
+    hidden, pooled, joined, pre = (
+        [hid_0, hid_1, hid_2], [pool_0, pool_1, pool_2], [join_0, join_1, join_2], [pre_0, pre_1],
+    )
+    top = LAYERS - 1
+
+    barrier = pltpu.get_barrier_semaphore()
+    for partner in place.partners():
+        pl.semaphore_signal(barrier, inc=1, device_id=partner, device_id_type=MESH)
+
+    feat_copy = pltpu.make_async_copy(feat_hbm, feat, feat_sem)
+    feat_copy.start()
+    win[z, y, x, c] = win_own[...].astype(bf16)
+    for layer in range(LAYERS):
+        weights[layer, 0, z, y, x, c] = pair_own[layer].astype(bf16)
+        weights[layer, 1, z, y, x, c] = proj_own[layer].astype(bf16)
+    head[z, y, x, c] = jnp.zeros(head.shape[4:], bf16)
+    head[z, y, x, c, :, 0:classes] = head_own[...].astype(bf16)
+
+    pl.semaphore_wait(barrier, 6)
+
+    regions = [
+        lambda zz, yy, xx, cc: win.at[zz, yy, xx, cc],
+        lambda zz, yy, xx, cc: weights.at[0, 0, zz, yy, xx, cc],
+        lambda zz, yy, xx, cc: weights.at[0, 1, zz, yy, xx, cc],
+        lambda zz, yy, xx, cc: weights.at[1, :, zz, yy, xx, cc],
+        lambda zz, yy, xx, cc: weights.at[2, :, zz, yy, xx, cc],
+        lambda zz, yy, xx, cc: head.at[zz, yy, xx, cc],
+    ]
+    gather_wires = [Wire(gather_send.at[at], gather_recv.at[at]) for at in range(len(regions))]
+    ga = [gather_steps(place, wire, region) for wire, region in zip(gather_wires, regions)]
+    step(*ga)
+
+    node_live = lax.broadcasted_iota(jnp.int32, (1, nodes), 1) < live[...]
+    slot = lax.broadcasted_iota(jnp.int32, nbr.shape, 0)
+    used = (slot < degree[...]) & (nbr[...] < live[...]) & node_live
+    edge_float = edge[...].astype(f32)
+    count_float = counts[...].astype(f32)
+    spread = jnp.maximum(jnp.sum(used.astype(f32), axis=0, keepdims=True), 1.0)
+    inverse[...] = jnp.where(node_live, 1.0 / count_float, 0.0)
+    scale[...] = count_float / (spread * COMMON)
+    sum_out[0, 0] = row_of_scalars(
+        [
+            jnp.sum(jnp.where(node_live, count_float, 0.0)),
+            jnp.sum(jnp.where(used, edge_float, 0.0)),
+            jnp.sum(inverse[...]),
+        ]
+    )
+
+    def keep_totals(block):
+        totals[...] = block
+
+    total_steps = sum_steps(
+        place, Wire(sum_send.at[0], sum_recv.at[0]), (sum_out, sum_in, sum_line), 0, keep_totals
+    )
+    step(total_steps)
+
+    term = jnp.where(used, COMMON / edge_float, 0.0)
+    summed = jnp.zeros(nbr.shape, f32)
+    for k in range(nbr.shape[0]):
+        summed = summed + jnp.where(nbr[k : k + 1, :] == nbr[...], term[k : k + 1, :], 0.0)
+    terms[...] = summed
+
+    @pl.loop(0, nodes // 256)
+    def _(block_at):
+        lanes = pl.ds(pl.multiple_of(block_at * 256, 256), 256)
+        ids = [jnp.broadcast_to(nbr[k : k + 1, lanes], (16, 256)).astype(jnp.int16) for k in range(8)]
+        values = [jnp.broadcast_to(terms[k : k + 1, lanes], (16, 256)).astype(bf16) for k in range(8)]
+
+        @pl.loop(0, nodes // 64)
+        def _(at):
+            for part in range(4):
+                row = pl.multiple_of(at * 64 + part * 16, 16)
+                own = (lax.broadcasted_iota(jnp.int32, (16, 256), 0) + row).astype(jnp.int16)
+                block = jnp.zeros((16, 256), bf16)
+                for k in range(8):
+                    block = jnp.where(ids[k] == own, values[k], block)
+                matrix[pl.ds(row, 16), lanes] = block
+
+        ticks(
+            block_at,
+            {
+                0: [total_steps],
+                1: [ga[0], ga[1], total_steps],
+                2: [ga[2]],
+                3: [ga[0], ga[1], total_steps],
+                4: [ga[3], ga[2]],
+                5: [ga[0], ga[1], total_steps],
+                6: [ga[4], ga[3], ga[2]],
+                7: [ga[0], ga[5]],
+            },
+        )
+
+    scale[...] = scale[...] * (totals[1:2, 0:1] / totals[0:1, 0:1])
+    feat_copy.wait()
+
+    def tile_at(at):
+        return pl.multiple_of(at * TILE, TILE)
+
+    @pl.loop(0, steps)
+    def _(at):
+        tile = pl.ds(tile_at(at), TILE)
+        hid_0[:, tile] = dot_nn(win[...].reshape(width, -1), feat[:, tile]).astype(bf16)
+
+    def pair_of(layer):
+        return weights[layer, 0].reshape(2 * width, width)
+
+    def proj_of(layer):
+        return weights[layer, 1].reshape(2 * width, width)
+
+    def layer_tile(layer, tile):
+        pooled[layer][:, tile] = (
+            dot_nn(hidden[layer][...], matrix[:, tile]) * scale[:, tile]
+        ).astype(bf16)
+        pair = pair_of(layer)
+        joined[layer][0:width, tile] = dot_nn(pair[:width], hidden[layer][:, tile]).astype(bf16)
+        joined[layer][width:, tile] = dot_nn(pair[width:], pooled[layer][:, tile]).astype(bf16)
+        return dot_nn(turned[...], joined[layer][:, tile])
+
+    forward_ticks = [
+        {0: [ga[3], ga[4], ga[5]], 1: [ga[3]], 2: [ga[4], ga[5]]},
+        {3: [ga[4], ga[5]]},
+    ]
+    step(ga[1], ga[2])
+    for layer in range(LAYERS - 1):
+        turned[...] = proj_of(layer).T
+
+        @pl.loop(0, steps)
+        def _(at, layer=layer):
+            before = tile_at(jnp.maximum(at - 1, 0))
+            norm_forward(pre[layer], active, hidden[layer + 1], before, before)
+            tile = pl.ds(tile_at(at), TILE)
+            pre[layer][:, tile] = layer_tile(layer, tile)
+            ticks(at, forward_ticks[layer])
+
+        final = tile_at(steps - 1)
+        norm_forward(pre[layer], active, hidden[layer + 1], final, final)
+
+    turned[...] = proj_of(top).T
+    head_grad[...] = jnp.zeros_like(head_grad)
+    losses[...] = jnp.zeros_like(losses)
+    class_row = lax.broadcasted_iota(jnp.int32, (48, TILE), 0)
+
+    def loss_tile(at):
+        start = tile_at(at)
+        tile = pl.ds(start, TILE)
+        head_rows = head[...].reshape(width, 128)
+        norm_forward(top_pre, active, last, 0, 0)
+        logits = jnp.where(class_row < classes, dot_nn(head_rows.T[0:48], last[...]), -1e30)
+        most = jnp.max(logits, axis=0, keepdims=True)
+        log_total = jnp.log(jnp.sum(jnp.exp(logits - most), axis=0, keepdims=True)) + most
+        target = class_row == labels[:, tile]
+        picked = jnp.sum(jnp.where(target, logits, 0.0), axis=0, keepdims=True)
+        loss = jnp.sum(inverse[:, tile] * (log_total - picked), axis=1, keepdims=True)
+        losses[...] = losses[...] + loss
+        weight = inverse[:, tile] / totals[2:3, 0:1]
+        grad_logits = (weight * (jnp.exp(logits - log_total) - target.astype(f32))).astype(bf16)
+        grad_logits = jnp.concatenate([grad_logits, jnp.zeros((80, TILE), bf16)], axis=0)
+        head_grad[...] = head_grad[...] + dot_nt(last[...], grad_logits)
+        back[...] = dot_nn(head_rows, grad_logits)
+        norm_backward(back, top_pre, active, slope, feat, 0, start)
+
+    @pl.loop(0, steps)
+    def _(at):
+        top_pre[...] = layer_tile(top, pl.ds(tile_at(at), TILE))
+        loss_tile(at)
+
+    hd_g[0] = head_grad[...].astype(bf16).reshape(hd_g.shape[1:])
+    sum_out[1, 0] = jnp.broadcast_to(losses[0:1, 0:1], (8, 128))
+
+    def keep_loss(block):
+        rows = lax.broadcasted_iota(jnp.int32, (8, 128), 0)
+        all_nodes = float(nodes * 32)
+        weight_mean = (totals[0:1, :] * totals[2:3, :]) / (all_nodes * all_nodes)
+        scal_out[...] = jnp.where(rows == 0, block / totals[2:3, :], weight_mean)
+
+    loss_steps = sum_steps(
+        place, Wire(sum_send.at[1], sum_recv.at[1]), (sum_out, sum_in, sum_line), 1, keep_loss
+    )
+
+    def keep_head(value):
+        ghead_out[...] = value[:, 0:classes]
+
+    head_steps = scatter_steps(
+        place, Wire(scatter_send.at[0], scatter_recv.at[0]),
+        (hd_g, hd_rc, hd_oh, hd_ih, hd_ocol, hd_icol, hd_oz, hd_iz), 0, keep_head,
+    )
+    step(loss_steps, head_steps)
+
+    def big_steps(chunk, slot, target, layer):
+        def keep(value):
+            target[layer] = value
+
+        return scatter_steps(
+            place, Wire(scatter_send.at[chunk], scatter_recv.at[chunk]),
+            (big_g, big_rc, big_oh, big_ih, big_ocol, big_icol, big_oz, big_iz), slot, keep,
+        )
+
+    def grad_block(slot, at, left, right):
+        rows = pl.ds(pl.multiple_of(at * 256, 256), 256)
+        big_g[slot, at] = dot_nt(left[rows, :], right).astype(bf16).reshape(big_g.shape[2:])
+
+    for layer in reversed(range(LAYERS)):
+        chunk = 1 + 2 * (top - layer)
+        grad = feat.at[0:width] if layer == top else hidden[layer + 1]
+        beside = [loss_steps, head_steps] if layer == top else []
+
+        @pl.loop(0, 4)
+        def _(at, layer=layer, grad=grad):
+            grad_block(0, at, joined[layer], grad[...])
+
+        proj_steps = big_steps(chunk, 0, gproj_out, layer)
+        step(proj_steps, *beside)
+
+        @pl.loop(0, steps)
+        def _(at, layer=layer, grad=grad, proj_steps=proj_steps, beside=beside):
+            tile = pl.ds(tile_at(at), TILE)
+            joined[layer][:, tile] = dot_nn(proj_of(layer), grad[:, tile]).astype(bf16)
+            ticks(at, {1: [proj_steps] + beside, 3: [proj_steps] + beside})
+
+        if layer == top:
+            feat_copy = pltpu.make_async_copy(feat_hbm, feat, feat_sem)
+            feat_copy.start()
+
+        @pl.loop(0, 2)
+        def _(at, layer=layer):
+            grad_block(1, at, joined[layer], hidden[layer][...])
+
+        step(proj_steps, *beside)
+
+        @pl.loop(2, 4)
+        def _(at, layer=layer):
+            grad_block(1, at, joined[layer], pooled[layer][...])
+
+        step(proj_steps)
+        pair_steps = big_steps(chunk + 1, 1, gpair_out, layer)
+        step(pair_steps)
+        turned[...] = pair_of(layer).T
+
+        @pl.loop(0, steps)
+        def _(at, layer=layer):
+            tile = pl.ds(tile_at(at), TILE)
+            pooled[layer][:, tile] = (
+                dot_nn(turned[:, width:], joined[layer][width:, tile]) * scale[:, tile]
+            ).astype(bf16)
+
+        step(pair_steps)
+
+        @pl.loop(0, steps)
+        def _(at, layer=layer, pair_steps=pair_steps):
+            before = tile_at(jnp.maximum(at - 1, 0))
+            if layer > 0:
+                norm_backward(back, pre[layer - 1], active, slope, hidden[layer], before, before)
+            tile = pl.ds(tile_at(at), TILE)
+            value = dot_nn(turned[:, :width], joined[layer][:width, tile]) + dot_nt(
+                pooled[layer][...], matrix[tile, :]
+            )
+            if layer > 0:
+                back[...] = value
+            else:
+                hidden[layer][:, tile] = value.astype(bf16)
+            ticks(at, {0: [pair_steps], 1: [pair_steps], 2: [pair_steps]})
+
+        if layer > 0:
+            final = tile_at(steps - 1)
+            norm_backward(back, pre[layer - 1], active, slope, hidden[layer], final, final)
+
+    feat_copy.wait()
+    rows_in = width // 4
+
+    @pl.loop(0, 4)
+    def _(at):
+        rows = pl.ds(pl.multiple_of(at * rows_in, rows_in), rows_in)
+        in_g[0, at] = dot_nt(hid_0[rows, :], feat[...]).astype(bf16).reshape(in_g.shape[2:])
+
+    def keep_in(value):
+        gin_out[...] = value
+
+    in_steps = scatter_steps(
+        place, Wire(scatter_send.at[7], scatter_recv.at[7]),
+        (in_g, in_rc, in_oh, in_ih, in_ocol, in_icol, in_oz, in_iz), 0, keep_in,
+    )
+    for _ in in_steps:
+        pass
+    for wire in gather_wires:
+        wire.finish()
+
+
+def scatter_buffers(rows, columns, slots):
+    def buf(*shape):
+        return pltpu.VMEM((slots, *shape, rows, columns), bf16)
+
+    return [
+        buf(4, 2, 2, 2), buf(4, 2, 2), buf(2, 2), buf(2, 2), buf(2, 4), buf(2, 4), buf(3), buf(3),
+    ]
+
+
+def train(feat, nbr, edge, degree, counts, labels, live, win, pair, proj, head):
+    features, nodes = feat.shape
+    width = pair.shape[2]
+    classes = head.shape[1]
+    vmem = pl.BlockSpec(memory_space=pltpu.VMEM)
+    dma = pltpu.SemaphoreType.DMA
+    return pl.pallas_call(
+        train_kernel,
+        out_shape=[
+            jax.ShapeDtypeStruct(win.shape, f32),
+            jax.ShapeDtypeStruct(pair.shape, f32),
+            jax.ShapeDtypeStruct(proj.shape, f32),
+            jax.ShapeDtypeStruct(head.shape, f32),
+            jax.ShapeDtypeStruct((8, 128), f32),
+        ],
+        in_specs=[pl.BlockSpec(memory_space=pl.ANY)] + [vmem] * 10,
+        out_specs=[vmem] * 5,
+        scratch_shapes=[
+            pltpu.VMEM((nodes, nodes), bf16),
+            pltpu.VMEM((features, nodes), bf16),
+        ]
+        + [pltpu.VMEM((width, nodes), bf16)] * 3
+        + [pltpu.VMEM((width, nodes), bf16)] * 3
+        + [pltpu.VMEM((2 * width, nodes), bf16)] * 3
+        + [pltpu.VMEM((width, nodes), f32)] * 2
+        + [
+            pltpu.VMEM((4, 2, 2, 2, 16, features), bf16),
+            pltpu.VMEM((LAYERS, 2, 4, 2, 2, 2, 32, width), bf16),
+            pltpu.VMEM((4, 2, 2, 2, 16, 128), bf16),
+            pltpu.VMEM((width, 2 * width), bf16),
+            pltpu.VMEM((width, 128), f32),
+            pltpu.VMEM((1, nodes), f32),
+            pltpu.VMEM((1, nodes), f32),
+            pltpu.VMEM((8, nodes), f32),
+            pltpu.VMEM((8, 128), f32),
+            pltpu.VMEM((8, 128), f32),
+            pltpu.VMEM((width, TILE), f32),
+            pltpu.VMEM((width, TILE), f32),
+            pltpu.VMEM((width, TILE), bf16),
+            pltpu.VMEM((width, 128), f32),
+            pltpu.VMEM((width, 128), f32),
+        ]
+        + scatter_buffers(32, width, 2)
+        + scatter_buffers(16, features, 1)
+        + scatter_buffers(16, 128, 1)
+        + [
+            pltpu.VMEM((2, 3, 8, 128), f32),
+            pltpu.VMEM((2, 3, 8, 128), f32),
+            pltpu.VMEM((2, 4, 8, 128), f32),
+            dma((6, 11)), dma((6, 11)), dma((8, 8)), dma((8, 8)), dma((2, 6)), dma((2, 6)), dma,
+        ],
+        compiler_params=pltpu.CompilerParams(
+            collective_id=0, has_side_effects=True, vmem_limit_bytes=64 * 2**20
+        ),
+        cost_estimate=pl.CostEstimate(
+            flops=67 * 10**9, bytes_accessed=10**7, transcendentals=10**7
+        ),
+    )(feat, nbr, edge, degree, counts, labels, live, win, pair, proj, head)
+
+
+def update_kernel(*refs):
+    inputs, outs = refs[:16], refs[16:]
+    for at in range(4):
+        weight, first, second, grad = (inputs[at + 4 * kind][...] for kind in range(4))
+        new, first_new, second_new = adamw_update(weight, first, second, grad)
+        outs[at][...] = new
+        outs[4 + at][...] = first_new
+        outs[8 + at][...] = second_new
+        outs[12 + at][...] = new.astype(bf16)
+
+
+def update(weights, firsts, seconds, grads):
+    shapes = [jax.ShapeDtypeStruct(w.shape, f32) for w in weights]
+    vmem = pl.BlockSpec(memory_space=pltpu.VMEM)
+    return pl.pallas_call(
+        update_kernel,
+        out_shape=shapes * 3 + [jax.ShapeDtypeStruct(w.shape, bf16) for w in weights],
+        in_specs=[vmem] * 16,
+        out_specs=[vmem] * 16,
+    )(*weights, *firsts, *seconds, *grads)
+
+
+def turned_first(array):
+    return jnp.swapaxes(array, -1, -2)
+
+
+def body(
+    features, labels, neighbors, degree, node_counts, edge_counts, live_nodes,
+    input_weight, pair_weight, proj_weight, head_weight,
+    input_first, pair_first, proj_first, head_first,
+    input_second, pair_second, proj_second, head_second,
+):
+    def owned(input_w, pair_w, proj_w, head_w):
+        return (turned_first(input_w), turned_first(pair_w), proj_w, head_w)
+
+    weights = owned(input_weight, pair_weight, proj_weight, head_weight)
+    *grads, scalars = train(
+        turned_first(features), turned_first(neighbors), turned_first(edge_counts),
+        degree[None, :], node_counts[None, :], labels[None, :], live_nodes[None, :], *weights,
+    )
+    results = update(
+        weights,
+        owned(input_first, pair_first, proj_first, head_first),
+        owned(input_second, pair_second, proj_second, head_second),
+        grads,
+    )
+    placed = []
+    for kind in range(4):
+        placed += owned(*results[4 * kind : 4 * kind + 4])
+    return (scalars[0, 0], scalars[1, 0], *placed)
 
 
 def normalize(preact):
@@ -105,18 +786,7 @@
     return (grad_hidden, grad_pair, grad_proj)
 
 
-def adamw_update(weight, first, second, grad):
-    first_new = beta_first * first + (1.0 - beta_first) * grad
-    second_new = beta_second * second + (1.0 - beta_second) * grad * grad
-    first_hat = first_new / (1.0 - beta_first**STEP)
-    second_hat = second_new / (1.0 - beta_second**STEP)
-    weight_new = weight - learn_rate * (
-        first_hat / (jnp.sqrt(second_hat) + adam_eps) + decay_rate * weight
-    )
-    return (weight_new, first_new, second_new)
-
-
-def body(
+def plain_body(
     features,
     labels,
     neighbors,
@@ -239,8 +909,9 @@
         P(None, ("dp", "group"), None),
         P(("dp", "group"), None),
     )
+    fits = dict(mesh.shape) == {"dp": 8, "group": 4}
     return jax.shard_map(
-        body,
+        body if fits else plain_body,
         mesh=mesh,
         in_specs=placed,
         out_specs=(

time: 975 us -> 205 us (0.21)
  waiting for transfers between devices: 387 us -> 0 us
  matrix products: 268 us -> 0 us
  Pallas kernels: 0 us -> 202 us
  blocking collectives: 162 us -> 0 us
  other arithmetic: 102 us -> 0 us
  local copies, waits for them, and re-layouts: 29.4 us -> 1.27 us
  between operations: 20.8 us -> 1.49 us
    reduce_scatter x3 -> x0, waiting for transfers between devices: 283 us -> none  [the longest x1 141 us: body(): lax.psum_scatter(jnp.stack(pair_grads), ('dp', 'group'), scatter_dimensio...]
    dot_general x37 -> x0, matrix products: 268 us -> none  [the longest x3 89.6 us: layer_forward(): jnp.dot(matrix, hidden.astype(jnp.float32), precision=lax.Precision.HIGHE...]
    pallas_call x0 -> x2, Pallas kernels: none -> 202 us  [the longest x1 199 us: train(): pl.pallas_call(train_kernel, out_shape=[jax.ShapeDtypeStruct(win.shape, f...]
    unnamed x7 -> x0, waiting for transfers between devices: 104 us -> none
    all_gather x2 -> x0, blocking collectives: 82.1 us -> none  [the longest x1 43.6 us: body(): lax.all_gather(head_weight.astype(jnp.bfloat16), ('dp', 'group'), axis=0,...]
    psum x2 -> x0, blocking collectives: 79.4 us -> none  [the longest x1 42.2 us: body(): total_node, total_edge = lax.psum((node_local, edge_local), ('dp', 'group'))]
    dot_general x3 -> x0, other arithmetic: 58.8 us -> none  [layer_backward(): lax.dot_general(matrix, grad_pooled, (((0,), (0,)), ((), ())), precision=...]
    convert_element_type x13 -> x0, other arithmetic: 25.8 us -> none  [the longest x3 12.9 us: layer_backward(): grad_preact = pullback(grad_out)[0].astype(jnp.bfloat16)]
  transfers between devices with their start and end apart: 6 -> 0, of which waited for: 3 -> 0; matrix products, arithmetic and copies ran while one was open for 29% -> 0% of each run, Pallas kernels for 0% -> 0%
where the time goes in v1:
time: 205 us; the launch traced here: 204 us
  Pallas kernels  202 us (99%)
    pallas_call x1, Pallas kernels, train(): pl.pallas_call(train_kernel, out_shape=[jax.ShapeDtypeStruct(win.shape, f...  199 us

profile of v1, /device:TPU:0, one launch (start us, length us, event | category | flops | bytes accessed | tf_op | source)
XLA Modules:
  0.0 204.5 jit_solution(2387292802541468919)
XLA Ops:
  1.3 198.9 %shard_map.322 = (f32[16,602]{1,0:T(8,128)}, f32[3,32,512]{2,1,0:T(8,128)}, f32[3,32,512]{2,1,0:T(8,128)}, f32[16,41]{1,0:T(8,128)}, f32[8,128]{1,0:T(8,128)}) custom-call(bf16[602,2048]{1,0:T(8,128)(2,1)} %bitcast.32, s32[8,2048]{1,0:T(8,128)} %bitcast.37, s32[8,2048]{1,0:T(8,128)} %bitcast.38, s32[1,2048]{1,0:T(1,128)} %bitcast.43, s32[1,2048]{1,0:T(1,128)} %bitcast.44, ...), custom_call_target="tpu_custom_call" | custom-call | flops 67000000512 | bytes 10000000 | tf_op jit(solution)/shard_map/pallas_call | solution.py:593
  200.2 1.3 fusion
  201.5 2.8 %shard_map.323 = (f32[16,602]{1,0:T(8,128)}, f32[3,32,512]{2,1,0:T(8,128)}, f32[3,32,512]{2,1,0:T(8,128)}, f32[16,41]{1,0:T(8,128)}, f32[16,602]{1,0:T(8,128)}, ...) custom-call(f32[16,602]{1,0:T(8,128)} %bitcast.29, ...), custom_call_target="tpu_custom_call" | custom-call | tf_op jit(solution)/shard_map/pallas_call | solution.py:661

commit v2 on v1

--- a/solution.py
+++ b/solution.py
@@ -21,9 +21,10 @@
 f32 = jnp.float32
 bf16 = jnp.bfloat16
 TILE = 512
+WIDE = 1024
 ROWS = 64
-GELU_IN = 0.7978845608028654
-GELU_CUBE = 0.044715
+GATE_IN = 0.7978845608028654
+GATE_CUBE = GATE_IN * 0.044715
 
 
 def dot_nn(left, right):
@@ -85,10 +86,11 @@
     def arrived(self, at, target, device):
         self.copy(at, target, target, device).wait_recv()
 
-    def finish(self):
+    def finish(self, below=100):
         for sent in self.sent:
-            self.copy(*sent).wait_send()
-        self.sent = []
+            if sent[0] < below:
+                self.copy(*sent).wait_send()
+        self.sent = [sent for sent in self.sent if sent[0] >= below]
 
 
 def gather_steps(place, wire, region):
@@ -129,8 +131,8 @@
     yield
 
 
-def scatter_steps(place, wire, bufs, slot, store):
-    grads, from_core, out_half, in_half, out_col, in_col, out_z, in_z = bufs
+def scatter_steps(place, wire, bufs, slot, store, free=None, reuses=False, reused=False):
+    grads, from_core, out_half, in_half, out_col, in_col, out_z, in_z, own = bufs
     z, y, x, c = place.z, place.y, place.x, place.c
     fy, fx, fc = place.far_y, place.far_x, place.far_c
     low, high = slice(0, 2), slice(2, 4)
@@ -141,9 +143,20 @@
     def both(zs, yy, xx):
         return grads[slot, zs, yy, xx, c].astype(f32) + from_core[slot, zs, yy, xx].astype(f32)
 
+    def until_free(*partners):
+        if reuses:
+            for partner in partners:
+                pl.semaphore_wait(free.at[slot, partner], 1)
+
+    def set_free(*partners):
+        for partner, device in partners:
+            pl.semaphore_signal(free.at[slot, partner], inc=1, device_id=device, device_id_type=MESH)
+
+    until_free(0)
     wire.send(0, at(grads, slice(0, 4), slice(0, 2), slice(0, 2), fc), at(from_core), place.sibling)
     yield
     wire.arrived(0, at(from_core), place.sibling)
+    until_free(1, 2)
     out_half[slot, 0] = both(low, fy, fx).astype(bf16)
     wire.send(1, at(out_half, 0), at(in_half, 0), place.beside_x)
     out_half[slot, 1] = both(high, fy, fx).astype(bf16)
@@ -165,15 +178,22 @@
         beside = in_col[slot, 0, zz].astype(f32) + in_col[slot, 1, zz].astype(f32)
         return both(zz, y, x) + beside
 
+    until_free(3, 4, 5)
+    own[slot] = column(z)
     for step in range(3):
         out_z[slot, step] = column(place.later_z[step]).astype(bf16)
         wire.send(5 + step, at(out_z, step), at(in_z, step), place.to_z[step])
+    wire.finish(5)
+    if reused:
+        set_free((0, place.sibling))
     yield
     for step in range(3):
         wire.arrived(5 + step, at(in_z, step), place.from_z[step])
     others = in_z[slot, 0].astype(f32) + in_z[slot, 1].astype(f32) + in_z[slot, 2].astype(f32)
-    store(column(z) + others)
+    store(own[slot] + others)
     wire.finish()
+    if reused:
+        set_free(*enumerate([place.beside_x, place.beside_y] + place.from_z, 1))
     yield
 
 
@@ -215,53 +235,42 @@
 
 
 def gelu(pre):
-    bend = jnp.tanh(GELU_IN * (pre + GELU_CUBE * (pre * pre * pre)))
-    return 0.5 * pre * (1.0 + bend), bend
-
-
-def lane_chunks(tile):
-    for at in range(0, TILE, 128):
-        yield pl.ds(tile + at, 128), slice(at, at + 128)
+    square = pre * pre
+    gate = 0.5 * jnp.tanh(pre * (GATE_CUBE * square + GATE_IN)) + 0.5
+    return pre * gate, gate, square
 
 
 def row_chunks():
     return [slice(at, at + ROWS) for at in range(0, 512, ROWS)]
 
 
-def norm_forward(pre, active, out, at_pre, at_out):
-    for (lanes, _), (to_lanes, _) in zip(lane_chunks(at_pre), lane_chunks(at_out)):
-        square = jnp.zeros((ROWS, 128), f32)
-        for row in row_chunks():
-            value, _ = gelu(pre[row, lanes])
-            active[row, :] = value
-            square = square + value * value
-        square = jnp.sum(square, axis=0, keepdims=True)
-        scale = lax.rsqrt(square * (1.0 / 512) + norm_eps)
-        for row in row_chunks():
-            out[row, to_lanes] = (active[row, :] * scale).astype(bf16)
-
-
-def norm_backward(grad, pre, active, slope, out, at_pre, at_out):
-    for (lanes, inside), (to_lanes, _) in zip(lane_chunks(at_pre), lane_chunks(at_out)):
-        square = jnp.zeros((ROWS, 128), f32)
-        along = jnp.zeros((ROWS, 128), f32)
-        for row in row_chunks():
-            at = pre[row, lanes]
-            value, bend = gelu(at)
-            active[row, :] = value
-            slope[row, :] = 0.5 * (1.0 + bend) + (0.5 * GELU_IN) * at * (1.0 - bend * bend) * (
-                1.0 + (3.0 * GELU_CUBE) * (at * at)
-            )
-            square = square + value * value
-            along = along + value * grad[row, inside]
-        square = jnp.sum(square, axis=0, keepdims=True)
-        along = jnp.sum(along, axis=0, keepdims=True) * (1.0 / 512)
-        scale = lax.rsqrt(square * (1.0 / 512) + norm_eps)
-        pull = scale * scale * scale * along
-        for row in row_chunks():
-            out[row, to_lanes] = (
-                slope[row, :] * (scale * grad[row, inside] - active[row, :] * pull)
-            ).astype(bf16)
+def norm_forward(pre, active, scales, out, lanes, scale_lanes):
+    square = jnp.zeros((ROWS, 128), f32)
+    for row in row_chunks():
+        value, _, _ = gelu(pre[row, lanes])
+        active[row, :] = value
+        square = square + value * value
+    scale = lax.rsqrt(jnp.sum(square, axis=0, keepdims=True) * (1.0 / 512) + norm_eps)
+    scales[:, scale_lanes] = scale
+    for row in row_chunks():
+        out[row, lanes] = (active[row, :] * scale).astype(bf16)
+
+
+def norm_backward(grad, pre, active, slope, scales, out, grad_lanes, pre_lanes, lanes):
+    scale = scales[:, lanes]
+    along = jnp.zeros((ROWS, 128), f32)
+    for row in row_chunks():
+        value, gate, square = gelu(pre[row, pre_lanes])
+        active[row, :] = value
+        slope[row, :] = gate + value * (
+            (1.0 - gate) * ((6.0 * GATE_CUBE) * square + 2.0 * GATE_IN)
+        )
+        along = along + value * grad[row, grad_lanes]
+    pull = scale * scale * scale * (jnp.sum(along, axis=0, keepdims=True) * (1.0 / 512))
+    for row in row_chunks():
+        out[row, lanes] = (
+            slope[row, :] * (scale * grad[row, grad_lanes] - active[row, :] * pull)
+        ).astype(bf16)
 
 
 def ticks(at, plan):
@@ -276,18 +285,18 @@
     feat_hbm, nbr, edge, degree, counts, labels, live, win_own, pair_own, proj_own, head_own,
     gin_out, gpair_out, gproj_out, ghead_out, scal_out,
     matrix, feat, hid_0, hid_1, hid_2, pool_0, pool_1, pool_2, join_0, join_1, join_2, pre_0, pre_1,
-    win, weights, head, turned, head_grad, scale, inverse, terms, totals, losses,
+    win, weights, head, turned, head_grad, scale, inverse, terms, totals, losses, scales,
     back, top_pre, last, active, slope,
-    big_g, big_rc, big_oh, big_ih, big_ocol, big_icol, big_oz, big_iz,
-    in_g, in_rc, in_oh, in_ih, in_ocol, in_icol, in_oz, in_iz,
-    hd_g, hd_rc, hd_oh, hd_ih, hd_ocol, hd_icol, hd_oz, hd_iz,
+    big_g, big_rc, big_oh, big_ih, big_ocol, big_icol, big_oz, big_iz, big_own,
+    in_g, in_rc, in_oh, in_ih, in_ocol, in_icol, in_oz, in_iz, in_own,
+    hd_g, hd_rc, hd_oh, hd_ih, hd_ocol, hd_icol, hd_oz, hd_iz, hd_own,
     sum_out, sum_in, sum_line,
-    gather_send, gather_recv, scatter_send, scatter_recv, sum_send, sum_recv, feat_sem,
+    gather_send, gather_recv, scatter_send, scatter_recv, sum_send, sum_recv, feat_sem, free,
 ):
     place = Place()
     z, y, x, c = place.z, place.y, place.x, place.c
     nodes, width, classes = nbr.shape[1], hid_0.shape[0], head_own.shape[1]
-    steps = nodes // TILE
+    steps, wide_steps, chunks = nodes // TILE, nodes // WIDE, nodes // 128
     hidden, pooled, joined, pre = (
         [hid_0, hid_1, hid_2], [pool_0, pool_1, pool_2], [join_0, join_1, join_2], [pre_0, pre_1],
     )
@@ -308,17 +317,18 @@
 
     pl.semaphore_wait(barrier, 6)
 
-    regions = [
-        lambda zz, yy, xx, cc: win.at[zz, yy, xx, cc],
-        lambda zz, yy, xx, cc: weights.at[0, 0, zz, yy, xx, cc],
-        lambda zz, yy, xx, cc: weights.at[0, 1, zz, yy, xx, cc],
-        lambda zz, yy, xx, cc: weights.at[1, :, zz, yy, xx, cc],
-        lambda zz, yy, xx, cc: weights.at[2, :, zz, yy, xx, cc],
-        lambda zz, yy, xx, cc: head.at[zz, yy, xx, cc],
-    ]
+    def region_of(layer, kind):
+        return lambda zz, yy, xx, cc: weights.at[layer, kind, zz, yy, xx, cc]
+
+    regions = (
+        [lambda zz, yy, xx, cc: win.at[zz, yy, xx, cc]]
+        + [region_of(layer, kind) for layer in range(LAYERS) for kind in range(2)]
+        + [lambda zz, yy, xx, cc: head.at[zz, yy, xx, cc]]
+    )
     gather_wires = [Wire(gather_send.at[at], gather_recv.at[at]) for at in range(len(regions))]
     ga = [gather_steps(place, wire, region) for wire, region in zip(gather_wires, regions)]
-    step(*ga)
+    to_in, to_pair_0, to_proj_0, to_pair_1, to_proj_1, to_pair_2, to_proj_2, to_head = ga
+    step(to_in, to_pair_0, to_proj_0, to_pair_1)
 
     node_live = lax.broadcasted_iota(jnp.int32, (1, nodes), 1) < live[...]
     slot = lax.broadcasted_iota(jnp.int32, nbr.shape, 0)
@@ -370,13 +380,13 @@
             block_at,
             {
                 0: [total_steps],
-                1: [ga[0], ga[1], total_steps],
-                2: [ga[2]],
-                3: [ga[0], ga[1], total_steps],
-                4: [ga[3], ga[2]],
-                5: [ga[0], ga[1], total_steps],
-                6: [ga[4], ga[3], ga[2]],
-                7: [ga[0], ga[5]],
+                1: [to_proj_1],
+                2: [to_in, total_steps],
+                3: [to_pair_2],
+                4: [to_proj_2, to_head, total_steps],
+                5: [to_pair_0],
+                6: [to_in],
+                7: [to_proj_0, to_pair_0, to_in, to_pair_1, total_steps, to_in],
             },
         )
 
@@ -386,10 +396,17 @@
     def tile_at(at):
         return pl.multiple_of(at * TILE, TILE)
 
-    @pl.loop(0, steps)
+    def wide(at):
+        return pl.ds(pl.multiple_of(at * WIDE, WIDE), WIDE)
+
+    def chunk_at(at, start=0):
+        return pl.ds(pl.multiple_of(start + at * 128, 128), 128)
+
+    @pl.loop(0, wide_steps)
     def _(at):
-        tile = pl.ds(tile_at(at), TILE)
+        tile = wide(at)
         hid_0[:, tile] = dot_nn(win[...].reshape(width, -1), feat[:, tile]).astype(bf16)
+        ticks(at, {0: [to_proj_0], 1: [to_proj_1, to_pair_0]})
 
     def pair_of(layer):
         return weights[layer, 0].reshape(2 * width, width)
@@ -397,35 +414,64 @@
     def proj_of(layer):
         return weights[layer, 1].reshape(2 * width, width)
 
-    def layer_tile(layer, tile):
+    def pool_tile(layer, tile):
         pooled[layer][:, tile] = (
             dot_nn(hidden[layer][...], matrix[:, tile]) * scale[:, tile]
         ).astype(bf16)
+
+    def join_tile(layer, tile):
         pair = pair_of(layer)
         joined[layer][0:width, tile] = dot_nn(pair[:width], hidden[layer][:, tile]).astype(bf16)
         joined[layer][width:, tile] = dot_nn(pair[width:], pooled[layer][:, tile]).astype(bf16)
-        return dot_nn(turned[...], joined[layer][:, tile])
-
-    forward_ticks = [
-        {0: [ga[3], ga[4], ga[5]], 1: [ga[3]], 2: [ga[4], ga[5]]},
-        {3: [ga[4], ga[5]]},
+
+    pool_ticks = [
+        {0: [to_pair_1, to_proj_0, to_pair_2], 1: [to_proj_1, to_pair_0, to_proj_0, to_proj_2]},
+        {0: [to_pair_1, to_proj_1], 1: [to_proj_2, to_head]},
+        {},
     ]
-    step(ga[1], ga[2])
+    join_ticks = [
+        {0: [to_pair_1], 1: [to_head]},
+        {1: [to_head]},
+        {},
+    ]
+    pre_ticks = [
+        {0: [to_proj_1, to_pair_2]},
+        {},
+    ]
+    norm_ticks = [
+        {chunks // 2 - 1: [to_pair_2, to_proj_2, to_head]},
+        {chunks // 2 - 1: [to_pair_2, to_proj_2]},
+    ]
+
+    def pool_and_join(layer):
+        @pl.loop(0, wide_steps)
+        def _(at):
+            pool_tile(layer, wide(at))
+            ticks(at, pool_ticks[layer])
+
+        @pl.loop(0, wide_steps)
+        def _(at):
+            join_tile(layer, wide(at))
+            ticks(at, join_ticks[layer])
+
+        turned[...] = proj_of(layer).T
+
     for layer in range(LAYERS - 1):
-        turned[...] = proj_of(layer).T
-
-        @pl.loop(0, steps)
+        pool_and_join(layer)
+
+        @pl.loop(0, wide_steps)
         def _(at, layer=layer):
-            before = tile_at(jnp.maximum(at - 1, 0))
-            norm_forward(pre[layer], active, hidden[layer + 1], before, before)
-            tile = pl.ds(tile_at(at), TILE)
-            pre[layer][:, tile] = layer_tile(layer, tile)
-            ticks(at, forward_ticks[layer])
-
-        final = tile_at(steps - 1)
-        norm_forward(pre[layer], active, hidden[layer + 1], final, final)
-
-    turned[...] = proj_of(top).T
+            pre[layer][:, wide(at)] = dot_nn(turned[...], joined[layer][:, wide(at)])
+            ticks(at, pre_ticks[layer])
+
+        @pl.loop(0, chunks // 2)
+        def _(at, layer=layer):
+            for part in range(2):
+                lanes = chunk_at(at * 2 + part)
+                norm_forward(pre[layer], active, scales.at[layer], hidden[layer + 1], lanes, lanes)
+            ticks(at, norm_ticks[layer])
+
+    pool_and_join(top)
     head_grad[...] = jnp.zeros_like(head_grad)
     losses[...] = jnp.zeros_like(losses)
     class_row = lax.broadcasted_iota(jnp.int32, (48, TILE), 0)
@@ -434,7 +480,9 @@
         start = tile_at(at)
         tile = pl.ds(start, TILE)
         head_rows = head[...].reshape(width, 128)
-        norm_forward(top_pre, active, last, 0, 0)
+        for part in range(TILE // 128):
+            inside = slice(part * 128, part * 128 + 128)
+            norm_forward(top_pre, active, scales.at[top], last, inside, chunk_at(part, start))
         logits = jnp.where(class_row < classes, dot_nn(head_rows.T[0:48], last[...]), -1e30)
         most = jnp.max(logits, axis=0, keepdims=True)
         log_total = jnp.log(jnp.sum(jnp.exp(logits - most), axis=0, keepdims=True)) + most
@@ -447,11 +495,15 @@
         grad_logits = jnp.concatenate([grad_logits, jnp.zeros((80, TILE), bf16)], axis=0)
         head_grad[...] = head_grad[...] + dot_nt(last[...], grad_logits)
         back[...] = dot_nn(head_rows, grad_logits)
-        norm_backward(back, top_pre, active, slope, feat, 0, start)
+        for part in range(TILE // 128):
+            inside = slice(part * 128, part * 128 + 128)
+            norm_backward(
+                back, top_pre, active, slope, scales.at[top], feat.at[0:width], inside, inside, chunk_at(part, start)
+            )
 
     @pl.loop(0, steps)
     def _(at):
-        top_pre[...] = layer_tile(top, pl.ds(tile_at(at), TILE))
+        top_pre[...] = dot_nn(turned[...], joined[top][:, pl.ds(tile_at(at), TILE)])
         loss_tile(at)
 
     hd_g[0] = head_grad[...].astype(bf16).reshape(hd_g.shape[1:])
@@ -472,7 +524,7 @@
 
     head_steps = scatter_steps(
         place, Wire(scatter_send.at[0], scatter_recv.at[0]),
-        (hd_g, hd_rc, hd_oh, hd_ih, hd_ocol, hd_icol, hd_oz, hd_iz), 0, keep_head,
+        (hd_g, hd_rc, hd_oh, hd_ih, hd_ocol, hd_icol, hd_oz, hd_iz, hd_own), 0, keep_head,
     )
     step(loss_steps, head_steps)
 
@@ -482,95 +534,92 @@
 
         return scatter_steps(
             place, Wire(scatter_send.at[chunk], scatter_recv.at[chunk]),
-            (big_g, big_rc, big_oh, big_ih, big_ocol, big_icol, big_oz, big_iz), slot, keep,
+            (big_g, big_rc, big_oh, big_ih, big_ocol, big_icol, big_oz, big_iz, big_own), slot, keep,
+            free=free, reuses=layer < top, reused=layer > 0,
         )
 
     def grad_block(slot, at, left, right):
-        rows = pl.ds(pl.multiple_of(at * 256, 256), 256)
-        big_g[slot, at] = dot_nt(left[rows, :], right).astype(bf16).reshape(big_g.shape[2:])
-
+        rows = pl.ds(pl.multiple_of(at * 512, 512), 512)
+        grad = dot_nt(left[rows, :], right).astype(bf16)
+        big_g[slot, pl.ds(at * 2, 2)] = grad.reshape(2, *big_g.shape[2:])
+
+    proj_before, pair_before = [], []
     for layer in reversed(range(LAYERS)):
         chunk = 1 + 2 * (top - layer)
         grad = feat.at[0:width] if layer == top else hidden[layer + 1]
-        beside = [loss_steps, head_steps] if layer == top else []
-
-        @pl.loop(0, 4)
-        def _(at, layer=layer, grad=grad):
+        loss_beside = [loss_steps] if layer == top else []
+        head_beside = [head_steps] if layer == top else []
+
+        @pl.loop(0, 2)
+        def _(at, layer=layer, grad=grad, plan={0: proj_before + pair_before + loss_beside}):
             grad_block(0, at, joined[layer], grad[...])
+            ticks(at, plan)
 
         proj_steps = big_steps(chunk, 0, gproj_out, layer)
-        step(proj_steps, *beside)
-
-        @pl.loop(0, steps)
-        def _(at, layer=layer, grad=grad, proj_steps=proj_steps, beside=beside):
-            tile = pl.ds(tile_at(at), TILE)
-            joined[layer][:, tile] = dot_nn(proj_of(layer), grad[:, tile]).astype(bf16)
-            ticks(at, {1: [proj_steps] + beside, 3: [proj_steps] + beside})
+        step(proj_steps, *loss_beside, *head_beside)
+
+        @pl.loop(0, wide_steps)
+        def _(at, layer=layer, grad=grad, plan={1: [proj_steps] + pair_before + loss_beside + head_beside}):
+            joined[layer][:, wide(at)] = dot_nn(proj_of(layer), grad[:, wide(at)]).astype(bf16)
+            ticks(at, plan)
 
         if layer == top:
             feat_copy = pltpu.make_async_copy(feat_hbm, feat, feat_sem)
             feat_copy.start()
 
-        @pl.loop(0, 2)
+        grad_block(1, 0, joined[layer], hidden[layer][...])
+        grad_block(1, 1, joined[layer], pooled[layer][...])
+        pair_steps = big_steps(chunk + 1, 1, gpair_out, layer)
+        step(pair_steps, proj_steps, *loss_beside, *head_beside)
+        turned[...] = pair_of(layer).T
+
+        @pl.loop(0, wide_steps)
         def _(at, layer=layer):
-            grad_block(1, at, joined[layer], hidden[layer][...])
-
-        step(proj_steps, *beside)
-
-        @pl.loop(2, 4)
-        def _(at, layer=layer):
-            grad_block(1, at, joined[layer], pooled[layer][...])
-
-        step(proj_steps)
-        pair_steps = big_steps(chunk + 1, 1, gpair_out, layer)
-        step(pair_steps)
-        turned[...] = pair_of(layer).T
-
-        @pl.loop(0, steps)
-        def _(at, layer=layer):
-            tile = pl.ds(tile_at(at), TILE)
+            tile = wide(at)
             pooled[layer][:, tile] = (
                 dot_nn(turned[:, width:], joined[layer][width:, tile]) * scale[:, tile]
             ).astype(bf16)
 
-        step(pair_steps)
-
         @pl.loop(0, steps)
-        def _(at, layer=layer, pair_steps=pair_steps):
-            before = tile_at(jnp.maximum(at - 1, 0))
-            if layer > 0:
-                norm_backward(back, pre[layer - 1], active, slope, hidden[layer], before, before)
+        def _(at, layer=layer, plan={0: [pair_steps], 1: [proj_steps] + head_beside, 2: [pair_steps]}):
             tile = pl.ds(tile_at(at), TILE)
-            value = dot_nn(turned[:, :width], joined[layer][:width, tile]) + dot_nt(
-                pooled[layer][...], matrix[tile, :]
-            )
-            if layer > 0:
-                back[...] = value
+            back[...] = dot_nn(turned[:, :width], joined[layer][:width, tile])
+            back[...] += dot_nt(pooled[layer][...], matrix[tile, :])
+            if layer == 0:
+                hidden[layer][:, tile] = back[...].astype(bf16)
             else:
-                hidden[layer][:, tile] = value.astype(bf16)
-            ticks(at, {0: [pair_steps], 1: [pair_steps], 2: [pair_steps]})
-
-        if layer > 0:
-            final = tile_at(steps - 1)
-            norm_backward(back, pre[layer - 1], active, slope, hidden[layer], final, final)
+
+                @pl.loop(0, TILE // 256)
+                def _(part_at):
+                    for part in range(2):
+                        inside = chunk_at(part_at * 2 + part)
+                        lanes = chunk_at(part_at * 2 + part, at * TILE)
+                        norm_backward(
+                            back, pre[layer - 1], active, slope, scales.at[layer - 1], hidden[layer], inside, lanes, lanes
+                        )
+
+            ticks(at, plan)
+
+        proj_before, pair_before = [proj_steps], [pair_steps]
 
     feat_copy.wait()
-    rows_in = width // 4
-
-    @pl.loop(0, 4)
+    @pl.loop(0, 2)
     def _(at):
-        rows = pl.ds(pl.multiple_of(at * rows_in, rows_in), rows_in)
-        in_g[0, at] = dot_nt(hid_0[rows, :], feat[...]).astype(bf16).reshape(in_g.shape[2:])
+        rows = pl.ds(pl.multiple_of(at * 256, 256), 256)
+        in_g[0, pl.ds(at * 2, 2)] = dot_nt(hid_0[rows, :], feat[...]).astype(bf16).reshape(2, *in_g.shape[2:])
 
     def keep_in(value):
         gin_out[...] = value
 
     in_steps = scatter_steps(
         place, Wire(scatter_send.at[7], scatter_recv.at[7]),
-        (in_g, in_rc, in_oh, in_ih, in_ocol, in_icol, in_oz, in_iz), 0, keep_in,
-    )
-    for _ in in_steps:
-        pass
+        (in_g, in_rc, in_oh, in_ih, in_ocol, in_icol, in_oz, in_iz, in_own), 0, keep_in,
+    )
+    step(in_steps, *proj_before)
+    step(in_steps, *pair_before)
+    step(in_steps)
+    step(in_steps, *pair_before)
+    step(in_steps)
     for wire in gather_wires:
         wire.finish()
 
@@ -581,6 +630,7 @@
 
     return [
         buf(4, 2, 2, 2), buf(4, 2, 2), buf(2, 2), buf(2, 2), buf(2, 4), buf(2, 4), buf(3), buf(3),
+        pltpu.VMEM((slots, rows, columns), f32),
     ]
 
 
@@ -620,6 +670,7 @@
             pltpu.VMEM((8, nodes), f32),
             pltpu.VMEM((8, 128), f32),
             pltpu.VMEM((8, 128), f32),
+            pltpu.VMEM((LAYERS, 1, nodes), f32),
             pltpu.VMEM((width, TILE), f32),
             pltpu.VMEM((width, TILE), f32),
             pltpu.VMEM((width, TILE), bf16),
@@ -633,7 +684,8 @@
             pltpu.VMEM((2, 3, 8, 128), f32),
             pltpu.VMEM((2, 3, 8, 128), f32),
             pltpu.VMEM((2, 4, 8, 128), f32),
-            dma((6, 11)), dma((6, 11)), dma((8, 8)), dma((8, 8)), dma((2, 6)), dma((2, 6)), dma,
+            dma((8, 11)), dma((8, 11)), dma((8, 8)), dma((8, 8)), dma((2, 6)), dma((2, 6)), dma,
+            pltpu.SemaphoreType.REGULAR((2, 6)),
         ],
         compiler_params=pltpu.CompilerParams(
             collective_id=0, has_side_effects=True, vmem_limit_bytes=64 * 2**20

time: 205 us -> 156 us (0.76)
  Pallas kernels: 202 us -> 153 us
    pallas_call x1, Pallas kernels: 199 us -> 150 us  [train(): pl.pallas_call(train_kernel, out_shape=[jax.ShapeDtypeStruct(win.shape, f...]
where the time goes in v2:
time: 156 us; the launch traced here: 155 us
  Pallas kernels  153 us (98%)
    pallas_call x1, Pallas kernels, train(): pl.pallas_call(train_kernel, out_shape=[jax.ShapeDtypeStruct(win.shape, f...  150 us

profile of v2, /device:TPU:0, one launch (start us, length us, event | category | flops | bytes accessed | tf_op | source)
XLA Modules:
  0.0 155.5 jit_solution(7156305780247943230)
XLA Ops:
  1.3 149.9 %shard_map.322 = (f32[16,602]{1,0:T(8,128)}, f32[3,32,512]{2,1,0:T(8,128)}, f32[3,32,512]{2,1,0:T(8,128)}, f32[16,41]{1,0:T(8,128)}, f32[8,128]{1,0:T(8,128)}) custom-call(bf16[602,2048]{1,0:T(8,128)(2,1)} %bitcast.32, s32[8,2048]{1,0:T(8,128)} %bitcast.37, s32[8,2048]{1,0:T(8,128)} %bitcast.38, s32[1,2048]{1,0:T(1,128)} %bitcast.43, s32[1,2048]{1,0:T(1,128)} %bitcast.44, ...), custom_call_target="tpu_custom_call" | custom-call | flops 67000000512 | bytes 10000000 | tf_op jit(solution)/shard_map/pallas_call | solution.py:643
  151.2 1.3 fusion
  152.5 2.8 %shard_map.323 = (f32[16,602]{1,0:T(8,128)}, f32[3,32,512]{2,1,0:T(8,128)}, f32[3,32,512]{2,1,0:T(8,128)}, f32[16,41]{1,0:T(8,128)}, f32[16,602]{1,0:T(8,128)}, ...) custom-call(f32[16,602]{1,0:T(8,128)} %bitcast.29, ...), custom_call_target="tpu_custom_call" | custom-call | tf_op jit(solution)/shard_map/pallas_call | solution.py:713

commit v3 on v2

--- a/solution.py
+++ b/solution.py
@@ -22,6 +22,7 @@
 bf16 = jnp.bfloat16
 TILE = 512
 WIDE = 1024
+SPLIT = 384
 ROWS = 64
 GATE_IN = 0.7978845608028654
 GATE_CUBE = GATE_IN * 0.044715
@@ -221,9 +222,78 @@
     yield
 
 
-def step(*generators):
-    for generator in generators:
-        next(generator)
+PLAN = {
+    ("start", 0): ("ia", "ib",),
+    ("slots", 0): ("tot",),
+    ("build", 0): ("tot",),
+    ("build", 1): ("ia", "p0",),
+    ("build", 2): ("ib", "q0",),
+    ("build", 3): ("tot",),
+    ("build", 5): ("ia",),
+    ("build", 6): ("ib", "tot",),
+    ("build", 7): ("p0", "p1", "ia", "ib", "ia", "tot", "ib",),
+    ("first", 0): ("q0", "q1",),
+    ("first", 1): ("p0",),
+    ("pool0", 0): ("p1", "p2",),
+    ("pool0", 1): ("p0", "q0", "q1", "q2", "p0",),
+    ("join0", 0): ("p1", "p2", "wh",),
+    ("join0", 1): ("q0", "q0",),
+    ("pre0", 0): ("q1", "q2", "wh",),
+    ("pre0", 1): ("p1",),
+    ("norm0", 6): ("p2",),
+    ("pool1", 0): ("q1",),
+    ("pool1", 1): ("q2", "wh", "p1",),
+    ("join1", 0): ("p2",),
+    ("join1", 1): ("q1",),
+    ("pre1", 0): ("q2", "wh",),
+    ("pool2", 1): ("p2",),
+    ("join2", 1): ("q2", "wh",),
+    ("loss", 0): ("rh", "los",),
+    ("A2", 0): ("rh", "los",),
+    ("A2", 1): ("P2",),
+    ("B2", 0): ("rh", "los",),
+    ("B2", 1): ("P2",),
+    ("C2", 0): ("rh", "los",),
+    ("C2", 1): ("Q2",),
+    ("D2", 0): ("P2", "rh", "los",),
+    ("D2", 1): ("Q2",),
+    ("E2", 1): ("P2", "Q2",),
+    ("E2", 3): ("P2", "Q2",),
+    ("A1", 1): ("P1",),
+    ("B1", 1): ("Q2", "P1",),
+    ("C1", 1): ("Q1",),
+    ("D1", 0): ("P1",),
+    ("E1", 0): ("Q1",),
+    ("E1", 1): ("P1",),
+    ("E1", 2): ("Q1",),
+    ("E1", 3): ("P1",),
+    ("A0", 1): ("Q1", "P0",),
+    ("B0", 1): ("P0",),
+    ("C0", 1): ("Q1", "Q0",),
+    ("D0", 0): ("P0",),
+    ("E0", 0): ("Q0",),
+    ("E0", 2): ("P0",),
+    ("E0", 3): ("Q0",),
+    ("inputs", 0): ("ra",),
+    ("inputs", 1): ("rb", "ra", "P0", "rb", "Q0", "ra", "rb", "ra", "rb", "Q0", "ra", "rb",),
+}
+
+
+class Moves:
+    def __init__(self):
+        self.under_way = {}
+
+    def play(self, label, at=0):
+        for name in PLAN.get((label, at), ()):
+            next(self.under_way[name])
+
+    def after(self, label, at, count):
+        for when in range(count):
+            if (label, when) in PLAN:
+
+                @pl.when(at == when)
+                def _(when=when):
+                    self.play(label, when)
 
 
 def row_of_scalars(values):
@@ -273,14 +343,6 @@
         ).astype(bf16)
 
 
-def ticks(at, plan):
-    for when, generators in plan.items():
-
-        @pl.when(at == when)
-        def _(generators=generators):
-            step(*generators)
-
-
 def train_kernel(
     feat_hbm, nbr, edge, degree, counts, labels, live, win_own, pair_own, proj_own, head_own,
     gin_out, gpair_out, gproj_out, ghead_out, scal_out,
@@ -288,7 +350,8 @@
     win, weights, head, turned, head_grad, scale, inverse, terms, totals, losses, scales,
     back, top_pre, last, active, slope,
     big_g, big_rc, big_oh, big_ih, big_ocol, big_icol, big_oz, big_iz, big_own,
-    in_g, in_rc, in_oh, in_ih, in_ocol, in_icol, in_oz, in_iz, in_own,
+    ina_g, ina_rc, ina_oh, ina_ih, ina_ocol, ina_icol, ina_oz, ina_iz, ina_own,
+    inb_g, inb_rc, inb_oh, inb_ih, inb_ocol, inb_icol, inb_oz, inb_iz, inb_own,
     hd_g, hd_rc, hd_oh, hd_ih, hd_ocol, hd_icol, hd_oz, hd_iz, hd_own,
     sum_out, sum_in, sum_line,
     gather_send, gather_recv, scatter_send, scatter_recv, sum_send, sum_recv, feat_sem, free,
@@ -300,7 +363,7 @@
     hidden, pooled, joined, pre = (
         [hid_0, hid_1, hid_2], [pool_0, pool_1, pool_2], [join_0, join_1, join_2], [pre_0, pre_1],
     )
-    top = LAYERS - 1
+    top, features = LAYERS - 1, feat.shape[0]
 
     barrier = pltpu.get_barrier_semaphore()
     for partner in place.partners():
@@ -320,15 +383,23 @@
     def region_of(layer, kind):
         return lambda zz, yy, xx, cc: weights.at[layer, kind, zz, yy, xx, cc]
 
-    regions = (
-        [lambda zz, yy, xx, cc: win.at[zz, yy, xx, cc]]
-        + [region_of(layer, kind) for layer in range(LAYERS) for kind in range(2)]
-        + [lambda zz, yy, xx, cc: head.at[zz, yy, xx, cc]]
-    )
-    gather_wires = [Wire(gather_send.at[at], gather_recv.at[at]) for at in range(len(regions))]
-    ga = [gather_steps(place, wire, region) for wire, region in zip(gather_wires, regions)]
-    to_in, to_pair_0, to_proj_0, to_pair_1, to_proj_1, to_pair_2, to_proj_2, to_head = ga
-    step(to_in, to_pair_0, to_proj_0, to_pair_1)
+    def region_of_input(columns):
+        return lambda zz, yy, xx, cc: win.at[zz, yy, xx, cc, :, columns]
+
+    regions = {
+        "ia": region_of_input(slice(0, SPLIT)),
+        "ib": region_of_input(slice(SPLIT, features)),
+        "wh": lambda zz, yy, xx, cc: head.at[zz, yy, xx, cc],
+    }
+    for layer in range(LAYERS):
+        regions[f"p{layer}"] = region_of(layer, 0)
+        regions[f"q{layer}"] = region_of(layer, 1)
+    moves = Moves()
+    gather_wires = []
+    for at, (name, region) in enumerate(regions.items()):
+        gather_wires.append(Wire(gather_send.at[at], gather_recv.at[at]))
+        moves.under_way[name] = gather_steps(place, gather_wires[-1], region)
+    moves.play("start")
 
     node_live = lax.broadcasted_iota(jnp.int32, (1, nodes), 1) < live[...]
     slot = lax.broadcasted_iota(jnp.int32, nbr.shape, 0)
@@ -349,10 +420,10 @@
     def keep_totals(block):
         totals[...] = block
 
-    total_steps = sum_steps(
+    moves.under_way["tot"] = sum_steps(
         place, Wire(sum_send.at[0], sum_recv.at[0]), (sum_out, sum_in, sum_line), 0, keep_totals
     )
-    step(total_steps)
+    moves.play("slots")
 
     term = jnp.where(used, COMMON / edge_float, 0.0)
     summed = jnp.zeros(nbr.shape, f32)
@@ -376,19 +447,7 @@
                     block = jnp.where(ids[k] == own, values[k], block)
                 matrix[pl.ds(row, 16), lanes] = block
 
-        ticks(
-            block_at,
-            {
-                0: [total_steps],
-                1: [to_proj_1],
-                2: [to_in, total_steps],
-                3: [to_pair_2],
-                4: [to_proj_2, to_head, total_steps],
-                5: [to_pair_0],
-                6: [to_in],
-                7: [to_proj_0, to_pair_0, to_in, to_pair_1, total_steps, to_in],
-            },
-        )
+        moves.after("build", block_at, nodes // 256)
 
     scale[...] = scale[...] * (totals[1:2, 0:1] / totals[0:1, 0:1])
     feat_copy.wait()
@@ -406,7 +465,7 @@
     def _(at):
         tile = wide(at)
         hid_0[:, tile] = dot_nn(win[...].reshape(width, -1), feat[:, tile]).astype(bf16)
-        ticks(at, {0: [to_proj_0], 1: [to_proj_1, to_pair_0]})
+        moves.after("first", at, wide_steps)
 
     def pair_of(layer):
         return weights[layer, 0].reshape(2 * width, width)
@@ -424,35 +483,16 @@
         joined[layer][0:width, tile] = dot_nn(pair[:width], hidden[layer][:, tile]).astype(bf16)
         joined[layer][width:, tile] = dot_nn(pair[width:], pooled[layer][:, tile]).astype(bf16)
 
-    pool_ticks = [
-        {0: [to_pair_1, to_proj_0, to_pair_2], 1: [to_proj_1, to_pair_0, to_proj_0, to_proj_2]},
-        {0: [to_pair_1, to_proj_1], 1: [to_proj_2, to_head]},
-        {},
-    ]
-    join_ticks = [
-        {0: [to_pair_1], 1: [to_head]},
-        {1: [to_head]},
-        {},
-    ]
-    pre_ticks = [
-        {0: [to_proj_1, to_pair_2]},
-        {},
-    ]
-    norm_ticks = [
-        {chunks // 2 - 1: [to_pair_2, to_proj_2, to_head]},
-        {chunks // 2 - 1: [to_pair_2, to_proj_2]},
-    ]
-
     def pool_and_join(layer):
         @pl.loop(0, wide_steps)
         def _(at):
             pool_tile(layer, wide(at))
-            ticks(at, pool_ticks[layer])
+            moves.after(f"pool{layer}", at, wide_steps)
 
         @pl.loop(0, wide_steps)
         def _(at):
             join_tile(layer, wide(at))
-            ticks(at, join_ticks[layer])
+            moves.after(f"join{layer}", at, wide_steps)
 
         turned[...] = proj_of(layer).T
 
@@ -462,14 +502,14 @@
         @pl.loop(0, wide_steps)
         def _(at, layer=layer):
             pre[layer][:, wide(at)] = dot_nn(turned[...], joined[layer][:, wide(at)])
-            ticks(at, pre_ticks[layer])
+            moves.after(f"pre{layer}", at, wide_steps)
 
         @pl.loop(0, chunks // 2)
         def _(at, layer=layer):
             for part in range(2):
                 lanes = chunk_at(at * 2 + part)
                 norm_forward(pre[layer], active, scales.at[layer], hidden[layer + 1], lanes, lanes)
-            ticks(at, norm_ticks[layer])
+            moves.after(f"norm{layer}", at, chunks // 2)
 
     pool_and_join(top)
     head_grad[...] = jnp.zeros_like(head_grad)
@@ -515,18 +555,18 @@
         weight_mean = (totals[0:1, :] * totals[2:3, :]) / (all_nodes * all_nodes)
         scal_out[...] = jnp.where(rows == 0, block / totals[2:3, :], weight_mean)
 
-    loss_steps = sum_steps(
+    moves.under_way["los"] = sum_steps(
         place, Wire(sum_send.at[1], sum_recv.at[1]), (sum_out, sum_in, sum_line), 1, keep_loss
     )
 
     def keep_head(value):
         ghead_out[...] = value[:, 0:classes]
 
-    head_steps = scatter_steps(
+    moves.under_way["rh"] = scatter_steps(
         place, Wire(scatter_send.at[0], scatter_recv.at[0]),
         (hd_g, hd_rc, hd_oh, hd_ih, hd_ocol, hd_icol, hd_oz, hd_iz, hd_own), 0, keep_head,
     )
-    step(loss_steps, head_steps)
+    moves.play("loss")
 
     def big_steps(chunk, slot, target, layer):
         def keep(value):
@@ -543,34 +583,31 @@
         grad = dot_nt(left[rows, :], right).astype(bf16)
         big_g[slot, pl.ds(at * 2, 2)] = grad.reshape(2, *big_g.shape[2:])
 
-    proj_before, pair_before = [], []
     for layer in reversed(range(LAYERS)):
         chunk = 1 + 2 * (top - layer)
         grad = feat.at[0:width] if layer == top else hidden[layer + 1]
-        loss_beside = [loss_steps] if layer == top else []
-        head_beside = [head_steps] if layer == top else []
+
+        moves.under_way[f"P{layer}"] = big_steps(chunk, 0, gproj_out, layer)
+        moves.under_way[f"Q{layer}"] = big_steps(chunk + 1, 1, gpair_out, layer)
 
         @pl.loop(0, 2)
-        def _(at, layer=layer, grad=grad, plan={0: proj_before + pair_before + loss_beside}):
+        def _(at, layer=layer, grad=grad):
             grad_block(0, at, joined[layer], grad[...])
-            ticks(at, plan)
-
-        proj_steps = big_steps(chunk, 0, gproj_out, layer)
-        step(proj_steps, *loss_beside, *head_beside)
+            moves.after(f"A{layer}", at, 2)
 
         @pl.loop(0, wide_steps)
-        def _(at, layer=layer, grad=grad, plan={1: [proj_steps] + pair_before + loss_beside + head_beside}):
+        def _(at, layer=layer, grad=grad):
             joined[layer][:, wide(at)] = dot_nn(proj_of(layer), grad[:, wide(at)]).astype(bf16)
-            ticks(at, plan)
+            moves.after(f"B{layer}", at, wide_steps)
 
         if layer == top:
             feat_copy = pltpu.make_async_copy(feat_hbm, feat, feat_sem)
             feat_copy.start()
 
         grad_block(1, 0, joined[layer], hidden[layer][...])
+        moves.play(f"C{layer}", 0)
         grad_block(1, 1, joined[layer], pooled[layer][...])
-        pair_steps = big_steps(chunk + 1, 1, gpair_out, layer)
-        step(pair_steps, proj_steps, *loss_beside, *head_beside)
+        moves.play(f"C{layer}", 1)
         turned[...] = pair_of(layer).T
 
         @pl.loop(0, wide_steps)
@@ -579,9 +616,10 @@
             pooled[layer][:, tile] = (
                 dot_nn(turned[:, width:], joined[layer][width:, tile]) * scale[:, tile]
             ).astype(bf16)
+            moves.after(f"D{layer}", at, wide_steps)
 
         @pl.loop(0, steps)
-        def _(at, layer=layer, plan={0: [pair_steps], 1: [proj_steps] + head_beside, 2: [pair_steps]}):
+        def _(at, layer=layer):
             tile = pl.ds(tile_at(at), TILE)
             back[...] = dot_nn(turned[:, :width], joined[layer][:width, tile])
             back[...] += dot_nt(pooled[layer][...], matrix[tile, :])
@@ -598,28 +636,32 @@
                             back, pre[layer - 1], active, slope, scales.at[layer - 1], hidden[layer], inside, lanes, lanes
                         )
 
-            ticks(at, plan)
-
-        proj_before, pair_before = [proj_steps], [pair_steps]
+            moves.after(f"E{layer}", at, steps)
+
+    def keep_in(columns):
+        def keep(value):
+            gin_out[:, columns] = value
+
+        return keep
 
     feat_copy.wait()
-    @pl.loop(0, 2)
-    def _(at):
-        rows = pl.ds(pl.multiple_of(at * 256, 256), 256)
-        in_g[0, pl.ds(at * 2, 2)] = dot_nt(hid_0[rows, :], feat[...]).astype(bf16).reshape(2, *in_g.shape[2:])
-
-    def keep_in(value):
-        gin_out[...] = value
-
-    in_steps = scatter_steps(
-        place, Wire(scatter_send.at[7], scatter_recv.at[7]),
-        (in_g, in_rc, in_oh, in_ih, in_ocol, in_icol, in_oz, in_iz, in_own), 0, keep_in,
-    )
-    step(in_steps, *proj_before)
-    step(in_steps, *pair_before)
-    step(in_steps)
-    step(in_steps, *pair_before)
-    step(in_steps)
+    for at, (name, bufs, columns) in enumerate(
+        [
+            ("ra", (ina_g, ina_rc, ina_oh, ina_ih, ina_ocol, ina_icol, ina_oz, ina_iz, ina_own), slice(0, SPLIT)),
+            ("rb", (inb_g, inb_rc, inb_oh, inb_ih, inb_ocol, inb_icol, inb_oz, inb_iz, inb_own), slice(SPLIT, features)),
+        ]
+    ):
+
+        @pl.loop(0, 2)
+        def _(half, bufs=bufs, columns=columns):
+            rows = pl.ds(pl.multiple_of(half * 256, 256), 256)
+            grad = dot_nt(hid_0[rows, :], feat[columns, :]).astype(bf16)
+            bufs[0][0, pl.ds(half * 2, 2)] = grad.reshape(2, *bufs[0].shape[2:])
+
+        moves.under_way[name] = scatter_steps(
+            place, Wire(scatter_send.at[7 + at], scatter_recv.at[7 + at]), bufs, 0, keep_in(columns)
+        )
+        moves.play("inputs", at)
     for wire in gather_wires:
         wire.finish()
 
@@ -678,13 +720,14 @@
             pltpu.VMEM((width, 128), f32),
         ]
         + scatter_buffers(32, width, 2)
-        + scatter_buffers(16, features, 1)
+        + scatter_buffers(16, SPLIT, 1)
+        + scatter_buffers(16, features - SPLIT, 1)
         + scatter_buffers(16, 128, 1)
         + [
             pltpu.VMEM((2, 3, 8, 128), f32),
             pltpu.VMEM((2, 3, 8, 128), f32),
             pltpu.VMEM((2, 4, 8, 128), f32),
-            dma((8, 11)), dma((8, 11)), dma((8, 8)), dma((8, 8)), dma((2, 6)), dma((2, 6)), dma,
+            dma((9, 11)), dma((9, 11)), dma((9, 8)), dma((9, 8)), dma((2, 6)), dma((2, 6)), dma,
             pltpu.SemaphoreType.REGULAR((2, 6)),
         ],
         compiler_params=pltpu.CompilerParams(
@@ -696,8 +739,10 @@
     )(feat, nbr, edge, degree, counts, labels, live, win, pair, proj, head)
 
 
-def update_kernel(*refs):
+def update_kernel(scalars, *refs):
     inputs, outs = refs[:16], refs[16:]
+    outs[16][0, 0] = scalars[0, 0]
+    outs[17][0, 0] = scalars[1, 0]
     for at in range(4):
         weight, first, second, grad = (inputs[at + 4 * kind][...] for kind in range(4))
         new, first_new, second_new = adamw_update(weight, first, second, grad)
@@ -707,15 +752,18 @@
         outs[12 + at][...] = new.astype(bf16)
 
 
-def update(weights, firsts, seconds, grads):
+def update(scalars, weights, firsts, seconds, grads):
     shapes = [jax.ShapeDtypeStruct(w.shape, f32) for w in weights]
     vmem = pl.BlockSpec(memory_space=pltpu.VMEM)
+    smem = pl.BlockSpec(memory_space=pltpu.SMEM)
     return pl.pallas_call(
         update_kernel,
-        out_shape=shapes * 3 + [jax.ShapeDtypeStruct(w.shape, bf16) for w in weights],
-        in_specs=[vmem] * 16,
-        out_specs=[vmem] * 16,
-    )(*weights, *firsts, *seconds, *grads)
+        out_shape=shapes * 3
+        + [jax.ShapeDtypeStruct(w.shape, bf16) for w in weights]
+        + [jax.ShapeDtypeStruct((1, 1), f32)] * 2,
+        in_specs=[smem] + [vmem] * 16,
+        out_specs=[vmem] * 16 + [smem] * 2,
+    )(scalars, *weights, *firsts, *seconds, *grads)
 
 
 def turned_first(array):
@@ -736,7 +784,8 @@
         turned_first(features), turned_first(neighbors), turned_first(edge_counts),
         degree[None, :], node_counts[None, :], labels[None, :], live_nodes[None, :], *weights,
     )
-    results = update(
+    *results, mean_loss, weight_mean = update(
+        scalars,
         weights,
         owned(input_first, pair_first, proj_first, head_first),
         owned(input_second, pair_second, proj_second, head_second),
@@ -745,7 +794,7 @@
     placed = []
     for kind in range(4):
         placed += owned(*results[4 * kind : 4 * kind + 4])
-    return (scalars[0, 0], scalars[1, 0], *placed)
+    return (mean_loss.reshape(()), weight_mean.reshape(()), *placed)
 
 
 def normalize(preact):

time: 156 us -> 145 us (0.929)
  Pallas kernels: 153 us -> 143 us
    pallas_call x1, Pallas kernels: 150 us -> 140 us  [train(): pl.pallas_call(train_kernel, out_shape=[jax.ShapeDtypeStruct(win.shape, f...]
where the time goes in v3:
time: 145 us
  Pallas kernels  143 us (99%)
  between operations  1.49 us (1%)
    pallas_call x1, Pallas kernels, train(): pl.pallas_call(train_kernel, out_shape=[jax.ShapeDtypeStruct(win.shape, f...  140 us
    pallas_call x1, Pallas kernels, update(): pl.pallas_call(update_kernel, out_shape=shapes * 3 + [jax.ShapeDtypeStruc...  2.93 us

profile of v3, /device:TPU:0, one launch (start us, length us, event | category | flops | bytes accessed | tf_op | source)
XLA Modules:
  0.0 144.6 jit_solution(11660872637549376201)
XLA Ops:
  1.3 140.2 %shard_map.322 = (f32[16,602]{1,0:T(8,128)}, f32[3,32,512]{2,1,0:T(8,128)}, f32[3,32,512]{2,1,0:T(8,128)}, f32[16,41]{1,0:T(8,128)}, f32[8,128]{1,0:T(8,128)}) custom-call(bf16[602,2048]{1,0:T(8,128)(2,1)} %bitcast.32, s32[8,2048]{1,0:T(8,128)} %bitcast.37, s32[8,2048]{1,0:T(8,128)} %bitcast.38, s32[1,2048]{1,0:T(1,128)} %bitcast.43, s32[1,2048]{1,0:T(1,128)} %bitcast.44, ...), custom_call_target="tpu_custom_call" | custom-call | flops 67000000512 | bytes 10000000 | tf_op jit(solution)/shard_map/pallas_call | solution.py:685
  141.5 2.9 %shard_map.323 = (f32[16,602]{1,0:T(8,128)}, f32[3,32,512]{2,1,0:T(8,128)}, f32[3,32,512]{2,1,0:T(8,128)}, f32[16,41]{1,0:T(8,128)}, f32[16,602]{1,0:T(8,128)}, ...) custom-call(f32[8,128]{1,0:T(8,128)} %get-tuple-element.41.scalars, ...), custom_call_target="tpu_custom_call" | custom-call | tf_op jit(solution)/shard_map/pallas_call | solution.py:759

commit v4 on v3

--- a/solution.py
+++ b/solution.py
@@ -401,9 +401,9 @@
         moves.under_way[name] = gather_steps(place, gather_wires[-1], region)
     moves.play("start")
 
-    node_live = lax.broadcasted_iota(jnp.int32, (1, nodes), 1) < live[...]
+    node_live = lax.broadcasted_iota(jnp.int32, (1, nodes), 1) < live[0]
     slot = lax.broadcasted_iota(jnp.int32, nbr.shape, 0)
-    used = (slot < degree[...]) & (nbr[...] < live[...]) & node_live
+    used = (slot < degree[...]) & (nbr[...] < live[0]) & node_live
     edge_float = edge[...].astype(f32)
     count_float = counts[...].astype(f32)
     spread = jnp.maximum(jnp.sum(used.astype(f32), axis=0, keepdims=True), 1.0)
@@ -691,7 +691,10 @@
             jax.ShapeDtypeStruct(head.shape, f32),
             jax.ShapeDtypeStruct((8, 128), f32),
         ],
-        in_specs=[pl.BlockSpec(memory_space=pl.ANY)] + [vmem] * 10,
+        in_specs=[pl.BlockSpec(memory_space=pl.ANY)]
+        + [vmem] * 5
+        + [pl.BlockSpec(memory_space=pltpu.SMEM)]
+        + [vmem] * 4,
         out_specs=[vmem] * 5,
         scratch_shapes=[
             pltpu.VMEM((nodes, nodes), bf16),
@@ -754,15 +757,21 @@
 
 def update(scalars, weights, firsts, seconds, grads):
     shapes = [jax.ShapeDtypeStruct(w.shape, f32) for w in weights]
-    vmem = pl.BlockSpec(memory_space=pltpu.VMEM)
     smem = pl.BlockSpec(memory_space=pltpu.SMEM)
+    blocks = [
+        pl.BlockSpec((1, *w.shape[1:]), lambda layer: (layer, 0, 0))
+        if w.ndim == 3
+        else pl.BlockSpec(w.shape, lambda layer: (0, 0))
+        for w in weights
+    ]
     return pl.pallas_call(
         update_kernel,
         out_shape=shapes * 3
         + [jax.ShapeDtypeStruct(w.shape, bf16) for w in weights]
         + [jax.ShapeDtypeStruct((1, 1), f32)] * 2,
-        in_specs=[smem] + [vmem] * 16,
-        out_specs=[vmem] * 16 + [smem] * 2,
+        grid=(LAYERS,),
+        in_specs=[smem] + blocks * 4,
+        out_specs=blocks * 4 + [smem] * 2,
     )(scalars, *weights, *firsts, *seconds, *grads)
 
 
@@ -782,7 +791,7 @@
     weights = owned(input_weight, pair_weight, proj_weight, head_weight)
     *grads, scalars = train(
         turned_first(features), turned_first(neighbors), turned_first(edge_counts),
-        degree[None, :], node_counts[None, :], labels[None, :], live_nodes[None, :], *weights,
+        degree[None, :], node_counts[None, :], labels[None, :], live_nodes, *weights,
     )
     *results, mean_loss, weight_mean = update(
         scalars,

time: 145 us -> 146 us (level)
  no operation moved by 1% of the time
where the time goes in v4:
time: 146 us; the launch traced here: 145 us
  Pallas kernels  144 us (99%)
  between operations  1.49 us (1%)
    pallas_call x1, Pallas kernels, train(): pl.pallas_call(train_kernel, out_shape=[jax.ShapeDtypeStruct(win.shape, f...  140 us
    pallas_call x1, Pallas kernels, update(): pl.pallas_call(update_kernel, out_shape=shapes * 3 + [jax.ShapeDtypeStruc...  3.68 us

profile of v4, /device:TPU:0, one launch (start us, length us, event | category | flops | bytes accessed | tf_op | source)
XLA Modules:
  0.0 145.2 jit_solution(12998787371874351210)
XLA Ops:
  1.3 140.1 %shard_map.322 = (f32[16,602]{1,0:T(8,128)}, f32[3,32,512]{2,1,0:T(8,128)}, f32[3,32,512]{2,1,0:T(8,128)}, f32[16,41]{1,0:T(8,128)}, f32[8,128]{1,0:T(8,128)}) custom-call(bf16[602,2048]{1,0:T(8,128)(2,1)} %bitcast.30, s32[8,2048]{1,0:T(8,128)} %bitcast.35, s32[8,2048]{1,0:T(8,128)} %bitcast.36, s32[1,2048]{1,0:T(1,128)} %bitcast.41, s32[1,2048]{1,0:T(1,128)} %bitcast.42, ...), custom_call_target="tpu_custom_call" | custom-call | flops 67000000512 | bytes 10000000 | tf_op jit(solution)/shard_map/pallas_call | solution.py:685
  141.4 3.7 %shard_map.323 = (f32[16,602]{1,0:T(8,128)}, f32[3,32,512]{2,1,0:T(8,128)}, f32[3,32,512]{2,1,0:T(8,128)}, f32[16,41]{1,0:T(8,128)}, f32[16,602]{1,0:T(8,128)}, ...) custom-call(f32[8,128]{1,0:T(8,128)} %get-tuple-element.41.scalars, ...), custom_call_target="tpu_custom_call" | custom-call | tf_op jit(solution)/shard_map/pallas_call | solution.py:767
